TPU v7x, 32 devices: a whole 2x2x4 slice. The times are simulated.
32 devices in a mesh: parts: 2 (over y), row: 4 (over z), col: 4 (over x, core).
Axes of the slice: x: 2, y: 2, z: 4, core: 2. Of those that a mesh axis runs over, the one named last changes fastest.
Arguments:
- amplitudes: bfloat16 [8, 100, 512, 512], P('parts', 'col', 'row'), parts along dimension 0, may hold values from -12 to 12
- integrals: bfloat16 [200, 512, 512], P(('parts', 'col'), 'row'), parts along dimension 0, may hold values from -0.109375 to 0.109375
- occ_irrep: int32 [200], P('parts'), parts along dimension 0, may hold values from 0 to 7, as said below
- vir_irrep: int32 [1024], P('parts'), parts along dimension 0, may hold values from 0 to 7, as said below
- screen: int32 [200, 8], P('parts'), parts along dimension 0, may hold values 0 or 1
- occ_energy: float32 [200], P('parts'), parts along dimension 0, may hold values from -1 to -0.3
- vir_energy: float32 [1024], P('parts'), parts along dimension 0, may hold values from 0.1 to 1
Outputs:
- update: float32 [512, 8, 512], P('row', 'parts', 'col'), parts along dimension 1
There are 2 independent parts, one for each index of `parts`. A program takes and returns all parts, laid end to end along the dimension named above; each array names one. Nothing has to cross between parts.
Inputs may be any that keep to these rules, and one draw needn't show every extreme that they name: `occ_irrep`: the labels never fall from one orbital to the next; the first is 0 and the last is 7. `vir_irrep`: the labels never fall from one orbital to the next and every label from 0 to 7 occurs; exactly one label covers 256 virtual orbitals, every other label fewer.
All inputs are finite; a program needn't handle non-finite values.
Results may differ from a plain program's by a relative error of at most 0.0003.
Values may be sent and summed in bfloat16 or wider, within the bound.
No kernel may reach another device: no remote copies, remote signals or barrier semaphores. Data moves between devices by JAX's collectives and lax.ppermute only.
A program may use at most 128 MiB of HBM per device.

v0:
```python
import jax
import jax.numpy as jnp
from jax import lax
from jax.sharding import PartitionSpec as P


def parity(first_label, second_label, third_label, fourth_label):
    return jnp.bitwise_xor(
        jnp.bitwise_xor(first_label, second_label), jnp.bitwise_xor(third_label, fourth_label)
    )


def on_device(amplitudes, integrals, occ_irrep, vir_irrep, screen, occ_energy, vir_energy):
    row_count = lax.axis_size("row")
    column_count = lax.axis_size("col")
    batch_size, occ_share, vir_share, vir_total = amplitudes.shape
    occ_total = occ_irrep.shape[0]
    occ_offset = lax.axis_index("col") * occ_share
    vir_offset = lax.axis_index("row") * vir_share
    occ_local = lax.dynamic_slice_in_dim(occ_irrep, occ_offset, occ_share)
    vir_local = lax.dynamic_slice_in_dim(vir_irrep, vir_offset, vir_share)
    pair_label = occ_irrep[batch_size]
    keep_amp = (
        parity(
            occ_irrep[:batch_size, None, None, None],
            occ_local[None, :, None, None],
            vir_local[None, None, :, None],
            vir_irrep[None, None, None, :],
        )
        == 0
    )
    amp_kept = jnp.where(keep_amp, amplitudes, jnp.zeros_like(amplitudes))
    irrep_codes = jnp.arange(8, dtype=jnp.int32)
    screen_rows = lax.dynamic_slice_in_dim(screen, occ_offset, occ_share, 0)
    screen_local = jnp.sum(
        screen_rows[:, None, :] * (vir_local[None, :, None] == irrep_codes).astype(jnp.int32),
        axis=2,
    )
    keep_int = (
        parity(
            occ_local[:, None, None], vir_local[None, :, None], pair_label, vir_irrep[None, None, :]
        )
        == 0
    ) & (screen_local[:, :, None] == 1)
    int_kept = jnp.where(keep_int, integrals, jnp.zeros_like(integrals))
    packed = amp_kept.reshape(batch_size, occ_share, vir_share, row_count, vir_share)
    packed = jnp.transpose(packed, (3, 1, 0, 4, 2)).reshape(
        row_count, occ_share, batch_size * vir_share * vir_share
    )
    arrived = lax.all_to_all(
        lax.all_to_all(packed, "row", split_axis=0, concat_axis=0, tiled=True),
        "col",
        split_axis=0,
        concat_axis=1,
        tiled=True,
    )
    block_count = row_count // column_count
    vir_columns = block_count * vir_share
    arranged = arrived.reshape(block_count, occ_total, batch_size, vir_share, vir_share)
    arranged = jnp.transpose(arranged, (1, 3, 2, 0, 4)).reshape(
        occ_total, vir_share, batch_size, vir_columns
    )
    cycle_whole = lax.dot_general(
        lax.all_gather(int_kept, "col", axis=0, tiled=True),
        arranged,
        (((0, 1), (0, 1)), ((), ())),
        preferred_element_type=jnp.float32,
    )
    cycle_mine = lax.psum_scatter(cycle_whole, "row", scatter_dimension=0, tiled=True)
    energy_cols = lax.dynamic_slice_in_dim(
        vir_energy, lax.axis_index("col") * vir_columns, vir_columns
    )
    energy_rows = lax.dynamic_slice_in_dim(vir_energy, vir_offset, vir_share)
    denominator = (
        occ_energy[:batch_size][None, :, None]
        + occ_energy[batch_size]
        - energy_cols[None, None, :]
        - energy_rows[:, None, None]
    )
    return cycle_mine / denominator


def solution(mesh):
    in_specs = (
        P("parts", "col", "row", None),
        P(("parts", "col"), "row", None),
        P("parts"),
        P("parts"),
        P("parts", None),
        P("parts"),
        P("parts"),
    )
    out_specs = P("row", "parts", "col")
    return jax.shard_map(
        on_device, mesh=mesh, in_specs=in_specs, out_specs=out_specs, check_vma=False
    )
```

profile of v0, /device:TPU:2, one launch (start us, length us, event | category | flops | bytes accessed | tf_op | source)
XLA Modules:
  0.0 719.4 jit_solution(14361143390792385288)
XLA Ops:
  6.5 0.0 copy-start
  6.5 0.8 dynamic_slice.16
  7.3 0.8 broadcast_xor_fusion
  8.1 0.7 dynamic_slice.15
  8.8 0.7 broadcast_xor_fusion.2
  9.5 11.0 %fusion = bf16[4,25,128,512]{3,2,1,0:T(8,128)(2,1)} fusion(bf16[4,25,128,512]{3,2,1,0:T(8,128)(2,1)} %param.7, s32[128,512]{1,0:T(8,128)S(1)} %broadcast_xor_fusion, s32[4,25]{1,0:T(4,128)S(1)} %broadcast_xor_fusion.2), kind=kLoop, calls=%fused_computation.1 | loop fusion | flops 19660800 | bytes 26476944 | tf_op jit(solution)/shard_map/jit(_where)/select_n | solution.py:32
  20.5 18.9 %reshape.174 = bf16[4,25,128,4,128]{4,3,2,1,0:T(4,128)(2,1)} reshape(bf16[4,25,128,512]{3,2,1,0:T(8,128)(2,1)} %fusion) | data formatting | bytes 26214400 | tf_op jit(solution)/shard_map/reshape | solution.py:46
  39.4 20.8 %copy.24 = bf16[4,25,128,4,128]{2,4,0,3,1:T(8,128)(2,1)} copy(bf16[4,25,128,4,128]{4,3,2,1,0:T(4,128)(2,1)} %reshape.174) | data formatting | bytes 26214400 | tf_op jit(solution)/shard_map/reshape | solution.py:46
  60.3 19.7 %reshape.175 = bf16[4,25,65536]{2,0,1:T(4,128)(2,1)} reshape(bf16[4,25,4,128,128]{4,3,2,0,1:T(8,128)(2,1)} %bitcast.25) | data formatting | bytes 26214400 | tf_op jit(solution)/shard_map/reshape | solution.py:47
  80.0 12.7 %copy.25 = bf16[4,25,65536]{2,1,0:T(8,128)(2,1)} copy(bf16[4,25,65536]{2,0,1:T(4,128)(2,1)} %reshape.175) | data formatting | bytes 26214400 | tf_op jit(solution)/shard_map/reshape | solution.py:47
  92.7 0.0 copy-start.5
  92.7 0.0 copy-start.3
  92.7 0.0 copy-start.2
  92.7 7.3 %all-to-all-start = ((bf16[4,25,65536]{2,1,0:T(8,128)(2,1)}), bf16[4,25,65536]{2,1,0:T(8,128)(2,1)}, u32[]{:S(2)}, u32[]{:S(2)}) async-start(bf16[4,25,65536]{2,1,0:T(8,128)(2,1)} %copy.25), calls=%async_computation | async-start | bytes 33554432 | tf_op jit(solution)/shard_map/all_to_all | solution.py:51
  100.0 0.0 all-gather.2.cloned.1.call-start
  100.0 0.0 copy-done.5
  100.0 0.6 slice.12
  100.6 0.0 copy-done
  100.6 0.1 constant_dynamic-slice_fusion
  100.7 0.1 copy.23
  100.8 0.1 multiply_reduce_fusion
  100.9 0.0 copy-done.3
  100.9 0.7 broadcast_xor_fusion.3
  101.6 0.1 broadcast_xor_fusion.1
  101.6 0.0 copy-done.2
  101.6 3.4 fusion.6
  105.1 0.0 all-gather.2.cloned.1.call-update
  105.1 0.0 reduce-scatter.2.cloned.1.call-start
  105.1 358.0 %all-to-all-done = bf16[4,25,65536]{2,1,0:T(8,128)(2,1)} async-done(((bf16[4,25,65536]{2,1,0:T(8,128)(2,1)}), bf16[4,25,65536]{2,1,0:T(8,128)(2,1)}, u32[]{:S(2)}, u32[]{:S(2)}) %all-to-all-start) | async-done | bytes 13107232 | tf_op jit(solution)/shard_map/all_to_all | solution.py:51
  463.1 192.9 %all_to_all.14 = bf16[4,25,65536]{2,1,0:T(8,128)(2,1)} all-to-all(bf16[4,25,65536]{2,1,0:T(8,128)(2,1)} %all-to-all-done), channel_id=1, replica_groups=mesh['parts'=2,'row'=4,'col'=4] {'col'}, dimensions={0} | all-to-all | bytes 26214400 | tf_op jit(solution)/shard_map/all_to_all | solution.py:50
  656.0 13.4 %reshape.176 = bf16[1,100,4,128,128]{4,3,2,1,0:T(8,128)(2,1)} reshape(bf16[4,25,65536]{2,1,0:T(8,128)(2,1)} %all_to_all.14) | data formatting | bytes 26214400 | tf_op jit(solution)/shard_map/reshape | solution.py:59
  669.4 0.0 copy-start.6
  669.4 0.0 copy-start.4
  669.4 0.0 all-gather.2.cloned.1.call-done
  669.4 0.0 copy-start.1
  669.4 14.6 %fusion.7 = f32[512,4,128]{2,0,1:T(8,128)} fusion(bf16[1,100,4,128,128]{4,3,2,1,0:T(8,128)(2,1)} %reshape.176, bf16[100,128,512]{2,1,0:T(8,128)(2,1)} %all-gather.2.cloned.1.call-done), kind=kOutput, calls=%fused_computation.9 | convolution fusion | flops 6710886400 | bytes 27262976 | tf_op jit(solution)/shard_map/dot_general | solution.py:63
  684.0 0.0 reduce-scatter.2.cloned.1.call-update
  684.1 0.0 copy-done.6
  684.1 0.6 slice.15
  684.6 0.0 copy-done.4
  684.6 0.1 fusion.13
  684.7 0.6 slice_add_fusion
  685.4 0.1 broadcast_subtract_fusion
  685.5 25.2 %reduce-scatter.2.cloned.1.call-done = f32[128,4,128]{2,0,1:T(8,128)} async-done(((f32[512,4,128]{2,0,1:T(8,128)}), f32[128,4,128]{2,0,1:T(8,128)}) %reduce-scatter.2.cloned.1.call-update) | async-done | bytes 262160 | tf_op jit(solution)/shard_map/reduce_scatter | solution.py:69
  710.7 1.1 subtract_divide_fusion
  711.7 0.9 copy.28
  712.6 0.0 copy-done.1
  (2 shorter events, 0.0 us)
Async XLA Ops:
  6.5 94.1 %copy-start = (s32[100,8]{0,1:T(8,128)S(1)}, s32[100,8]{0,1:T(8,128)}, u32[]{:S(2)}) copy-start(s32[100,8]{0,1:T(8,128)} %param.11) | copy-start | bytes 9604
  92.7 7.3 %copy-start.5 = (s32[100]{0:T(128)S(1)}, s32[100]{0:T(128)}, u32[]{:S(2)}) copy-start(s32[100]{0:T(128)} %param.9) | copy-start | bytes 1204
  92.7 8.2 %copy-start.3 = (s32[512]{0:T(512)S(1)}, s32[512]{0:T(512)}, u32[]{:S(2)}) copy-start(s32[512]{0:T(512)} %param.10) | copy-start | bytes 6148
  92.7 8.9 %copy-start.2 = (bf16[25,128,512]{2,1,0:T(8,128)(2,1)S(1)}, bf16[25,128,512]{2,1,0:T(8,128)(2,1)}, u32[]{:S(2)}) copy-start(bf16[25,128,512]{2,1,0:T(8,128)(2,1)} %param.8) | copy-start | bytes 9830404
  92.7 370.4 %all-to-all-start = ((bf16[4,25,65536]{2,1,0:T(8,128)(2,1)}), bf16[4,25,65536]{2,1,0:T(8,128)(2,1)}, u32[]{:S(2)}, u32[]{:S(2)}) async-start(bf16[4,25,65536]{2,1,0:T(8,128)(2,1)} %copy.25), calls=%async_computation | async-start | bytes 33554432 | tf_op jit(solution)/shard_map/all_to_all | solution.py:51
  100.0 569.4 %all-gather.2.cloned.1.call-start = ((), (), s32[]{:S(2)}) async-start(), calls=%async_computation.3 | async-start | bytes 16384000 | tf_op jit(solution)/shard_map/all_gather | solution.py:64
  105.1 605.6 %reduce-scatter.2.cloned.1.call-start = ((), (), s32[]{:S(2)}) async-start(), calls=%async_computation.4 | async-start | bytes 1310720 | tf_op jit(solution)/shard_map/reduce_scatter | solution.py:69
  669.4 14.7 %copy-start.6 = (f32[100]{0:T(128)S(1)}, f32[100]{0:T(128)}, u32[]{:S(2)}) copy-start(f32[100]{0:T(128)} %param.12) | copy-start | bytes 1204
  669.4 15.3 %copy-start.4 = (f32[512]{0:T(512)S(1)}, f32[512]{0:T(512)}, u32[]{:S(2)}) copy-start(f32[512]{0:T(512)} %param.13) | copy-start | bytes 6148
  669.4 43.2 %copy-start.1 = (s32[100,8]{0,1:T(8,128)S(1)}, s32[100,8]{0,1:T(8,128)}, u32[]{:S(2)}) copy-start(s32[100,8]{0,1:T(8,128)} %param.11) | copy-start | bytes 9604
Sparse Core Ops, SparseCore 0:
  105.2 85.2 all-gather.1
  684.2 26.4 reduce-scatter.1
where the time goes:
time: 723 us; the launch traced here: 719 us
  waiting for transfers between devices  383 us (53%)
  blocking collectives  193 us (27%)
  local copies, waits for them, and re-layouts  89.3 us (12%)
  other arithmetic  18.5 us (3%)
  matrix products  14.6 us (2%)
  between operations  13.5 us (2%)
  starting transfers between devices  7.34 us (1%)
    all_to_all x1, waiting for transfers between devices, on_device(): lax.all_to_all(packed, 'row', split_axis=0, concat_axis=0, tiled=True)  358 us
    all_to_all x1, blocking collectives, on_device(): lax.all_to_all(lax.all_to_all(packed, 'row', split_axis=0, concat_axis=0,...  193 us
    reshape x2, local copies, waits for them, and re-layouts, on_device(): amp_kept.reshape(batch_size, occ_share, vir_share, row_count, vir_share)  39.7 us
    reshape x2, local copies, waits for them, and re-layouts, on_device(): jnp.transpose(packed, (3, 1, 0, 4, 2))  32.4 us
    reduce_scatter x1, waiting for transfers between devices, on_device(): lax.psum_scatter(cycle_whole, 'row', scatter_dimension=0, tiled=True)  25.2 us
    dot_general x1, matrix products, on_device(): lax.dot_general(lax.all_gather(int_kept, 'col', axis=0, tiled=True), arra...  14.6 us
  transfers between devices with their start and end apart: 3, of which 2 were waited for; matrix products, arithmetic and copies ran while one was open for 3% of the time, Pallas kernels for 0%

commit v1 on v0

v1 whole, which is shorter than its diff:
```python
import jax
import jax.numpy as jnp
from jax import lax
from jax.experimental import pallas as pl
from jax.experimental.pallas import tpu as pltpu
from jax.sharding import PartitionSpec as P

FOLD = 256
K_STEP = 5


def folded_integrals(integrals, occ_local, vir_local, vir_irrep, pair_label, screen_rows):
    irrep_codes = jnp.arange(8, dtype=jnp.int32)
    screen_local = jnp.sum(
        screen_rows[:, None, :] * (vir_local[None, :, None] == irrep_codes).astype(jnp.int32),
        axis=2,
    )
    target = jnp.bitwise_xor(
        jnp.bitwise_xor(occ_local[:, None], vir_local[None, :]), pair_label
    )
    target = jnp.where(screen_local == 1, target, -1)
    keep = target[:, :, None] == vir_irrep[None, None, :]
    kept = jnp.where(keep, integrals, jnp.zeros_like(integrals))
    return kept[:, :, :FOLD] + kept[:, :, FOLD:]


def shard_product_kernel(
    block_ref, label_ref, amp_ref, int_ref, left_ref, right_ref, total_in_ref, total_ref, mix_ref
):
    step = pl.program_id(0)

    @pl.when(step == 0)
    def _():
        total_ref[...] = total_in_ref[...]
        mixed = jnp.bitwise_xor(left_ref[...], right_ref[...])
        mix_ref[...] = mixed.astype(jnp.float32).astype(jnp.bfloat16)

    rows = amp_ref.shape[0] * amp_ref.shape[2]
    mixed = mix_ref[...]
    pieces = []
    for j in range(amp_ref.shape[1]):
        label = label_ref[step * amp_ref.shape[1] + j].astype(jnp.float32)
        tile = amp_ref[:, j].reshape(rows, amp_ref.shape[3])
        wanted = jnp.full(mixed.shape, label, jnp.float32).astype(jnp.bfloat16)
        pieces.append(jnp.where(mixed == wanted, tile, jnp.zeros_like(tile)))
    lhs = jnp.concatenate(pieces, axis=1)
    rhs = int_ref[...].reshape(-1, int_ref.shape[2])
    total_ref[...] += jnp.dot(lhs, rhs, preferred_element_type=jnp.float32)


def shard_product(total, amplitudes, fold, block, labels, k_start, row_labels, col_labels):
    batch, _, share, _ = amplitudes.shape
    k_count, depth, width = fold.shape
    first = k_start // K_STEP
    rows = batch * share
    return pl.pallas_call(
        shard_product_kernel,
        grid_spec=pltpu.PrefetchScalarGridSpec(
            num_scalar_prefetch=2,
            grid=(k_count // K_STEP,),
            in_specs=[
                pl.BlockSpec((batch, K_STEP, share, depth), lambda k, s, l: (0, first + k, 0, s[0])),
                pl.BlockSpec((K_STEP, depth, width), lambda k, s, l: (k, 0, 0)),
                pl.BlockSpec((rows, 1), lambda k, s, l: (0, 0)),
                pl.BlockSpec((1, depth), lambda k, s, l: (0, s[0])),
                pl.BlockSpec((rows, width), lambda k, s, l: (0, 0)),
            ],
            out_specs=pl.BlockSpec((rows, width), lambda k, s, l: (0, 0)),
            scratch_shapes=[pltpu.VMEM((rows, depth), jnp.bfloat16)],
        ),
        out_shape=jax.ShapeDtypeStruct((rows, width), jnp.float32),
        input_output_aliases={6: 0},
        compiler_params=pltpu.CompilerParams(vmem_limit_bytes=32 * 1024 * 1024),
    )(block, labels, amplitudes, fold, row_labels, col_labels, total)


def finish(cycle, occ_irrep, vir_irrep, occ_energy, vir_energy, a_start, a_size, b_start, b_size, batch):
    label_a = lax.dynamic_slice_in_dim(vir_irrep, a_start, a_size)
    label_b = lax.dynamic_slice_in_dim(vir_irrep, b_start, b_size)
    energy_a = lax.dynamic_slice_in_dim(vir_energy, a_start, a_size)
    energy_b = lax.dynamic_slice_in_dim(vir_energy, b_start, b_size)
    target = jnp.bitwise_xor(
        jnp.bitwise_xor(occ_irrep[:batch, None], occ_irrep[batch]), label_a[None, :]
    )
    keep = label_b[:, None, None] == target[None, :, :]
    denominator = (
        occ_energy[:batch][None, :, None]
        + occ_energy[batch]
        - energy_a[None, None, :]
        - energy_b[:, None, None]
    )
    swapped = jnp.transpose(cycle, (2, 0, 1))
    return jnp.where(keep, swapped, 0.0) / denominator


def on_square(amplitudes, fold, occ_irrep, occ_local, vir_local, vir_irrep):
    rows_n = lax.axis_size("row")
    batch, occ_share, share, _ = amplitudes.shape
    row = lax.axis_index("row")
    col = lax.axis_index("col")
    row_labels = jnp.bitwise_xor(occ_irrep[:batch, None], vir_local[None, :]).reshape(-1, 1)
    col_labels = vir_irrep[None, :]
    chunks = [(0, 15), (15, occ_share)]
    total = jnp.zeros((batch * share, FOLD), jnp.float32)

    def add(total, part, source, chunk):
        block = jnp.clip(source, 0, rows_n - 1).astype(jnp.int32).reshape(1)
        return shard_product(
            total, amplitudes, part, block, occ_local[chunk[0]:chunk[1]], chunk[0], row_labels, col_labels
        )

    own = [fold[lo:hi] for lo, hi in chunks]
    rightward = [(i, i + 1) for i in range(rows_n - 1)]
    leftward = [(i + 1, i) for i in range(rows_n - 1)]
    from_left, from_right = own, own
    for distance in range(rows_n):
        if distance:
            from_left = [lax.ppermute(v, "row", rightward) for v in from_left]
            from_right = [lax.ppermute(v, "row", leftward) for v in from_right]
        for n, chunk in enumerate(chunks):
            total = add(total, from_left[n], row - distance, chunk)
            if distance:
                total = add(total, from_right[n], row + distance, chunk)
    half = col % 2
    chip = col // 2
    width = FOLD // 2
    total = total.reshape(batch, share, FOLD)
    kept = lax.dynamic_slice_in_dim(total, half * width, width, 2)
    sent = lax.dynamic_slice_in_dim(total, (1 - half) * width, width, 2)
    kept = kept + lax.ppermute(sent, "col", [(q, q ^ 1) for q in range(4)])
    pair = batch // 2
    mine = lax.dynamic_slice_in_dim(kept, chip * pair, pair, 0)
    sent = lax.dynamic_slice_in_dim(kept, (1 - chip) * pair, pair, 0)
    mine = mine + lax.ppermute(sent, "col", [(q, q ^ 2) for q in range(4)])
    places = [(r, q) for r in range(4) for q in range(4)]
    same = lax.ppermute(mine, ("row", "col"), [(r * 4 + q, q * 4 + r) for r, q in places])
    other = lax.ppermute(mine, ("row", "col"), [(r * 4 + q, (q ^ 2) * 4 + r) for r, q in places])
    upper = row // 2 == 1
    low = jnp.where(upper, other, same)
    high = jnp.where(upper, same, other)
    return jnp.concatenate([low, high], axis=0)


def on_any(amplitudes, fold, occ_irrep, occ_local, vir_local, vir_irrep):
    batch, _, share, vir_total = amplitudes.shape
    keep = (
        jnp.bitwise_xor(occ_irrep[:batch, None], occ_local[None, :])[:, :, None, None]
        == jnp.bitwise_xor(vir_local[:, None], vir_irrep[None, :])[None, None]
    )
    kept = jnp.where(keep, amplitudes, jnp.zeros_like(amplitudes))
    whole = lax.all_gather(fold, "row", axis=1, tiled=True)
    cycle = lax.dot_general(
        kept, whole, (((1, 3), (0, 1)), ((), ())), preferred_element_type=jnp.float32
    )
    cycle = lax.psum(cycle, "col")
    cycle = jnp.concatenate([cycle] * (vir_total // FOLD), axis=2)
    cycle = lax.all_to_all(cycle, "row", split_axis=2, concat_axis=1, tiled=True)
    a_size = vir_total // lax.axis_size("col")
    return lax.dynamic_slice_in_dim(cycle, lax.axis_index("col") * a_size, a_size, 1)


def on_device(amplitudes, integrals, occ_irrep, vir_irrep, screen, occ_energy, vir_energy):
    batch, occ_share, vir_share, vir_total = amplitudes.shape
    row = lax.axis_index("row")
    col = lax.axis_index("col")
    occ_local = lax.dynamic_slice_in_dim(occ_irrep, col * occ_share, occ_share)
    vir_local = lax.dynamic_slice_in_dim(vir_irrep, row * vir_share, vir_share)
    screen_rows = lax.dynamic_slice_in_dim(screen, col * occ_share, occ_share, 0)
    fold = folded_integrals(
        integrals, occ_local, vir_local, vir_irrep, occ_irrep[batch], screen_rows
    )
    square = lax.axis_size("row") == 4 and lax.axis_size("col") == 4
    form = on_square if square else on_any
    cycle = form(amplitudes, fold, occ_irrep, occ_local, vir_local, vir_irrep)
    a_size = vir_total // lax.axis_size("col")
    return finish(
        cycle, occ_irrep, vir_irrep, occ_energy, vir_energy,
        col * a_size, a_size, row * vir_share, vir_share, batch,
    )


def solution(mesh):
    in_specs = (
        P("parts", "col", "row", None),
        P(("parts", "col"), "row", None),
        P("parts"),
        P("parts"),
        P("parts", None),
        P("parts"),
        P("parts"),
    )
    out_specs = P("row", "parts", "col")
    return jax.shard_map(
        on_device, mesh=mesh, in_specs=in_specs, out_specs=out_specs, check_vma=False
    )
```

time: 723 us -> 171 us (0.24)
  waiting for transfers between devices: 383 us -> 62.7 us
  blocking collectives: 193 us -> 0 us
  local copies, waits for them, and re-layouts: 89.3 us -> 19.8 us
  Pallas kernels: 0 us -> 36.1 us
  starting transfers between devices: 7.34 us -> 43.4 us
  matrix products: 14.6 us -> 0 us
  between operations: 13.5 us -> 0.59 us
  other arithmetic: 18.5 us -> 6.13 us
    all_to_all x1 -> x0, waiting for transfers between devices: 358 us -> none  [on_device(): lax.all_to_all(packed, 'row', split_axis=0, concat_axis=0, tiled=True)]
    all_to_all x1 -> x0, blocking collectives: 193 us -> none  [on_device(): lax.all_to_all(lax.all_to_all(packed, 'row', split_axis=0, concat_axis=0,...]
    reshape x5 -> x0, local copies, waits for them, and re-layouts: 85.5 us -> none  [the longest x2 39.7 us: on_device(): amp_kept.reshape(batch_size, occ_share, vir_share, row_count, vir_share)]
    ppermute x0 -> x16, waiting for transfers between devices: none -> 62.7 us  [the longest x6 49.9 us: on_square(): from_left = [lax.ppermute(v, 'row', rightward) for v in from_left]]
    ppermute x0 -> x16, starting transfers between devices: none -> 43.4 us  [the longest x6 28.7 us: on_square(): from_left = [lax.ppermute(v, 'row', rightward) for v in from_left]]
    pallas_call x0 -> x14, Pallas kernels: none -> 36.1 us  [shard_product(): pl.pallas_call(shard_product_kernel, grid_spec=pltpu.PrefetchScalarGridSp...]
    reduce_scatter x1 -> x0, waiting for transfers between devices: 25.2 us -> none  [on_device(): lax.psum_scatter(cycle_whole, 'row', scatter_dimension=0, tiled=True)]
    unnamed x14 -> x42, local copies, waits for them, and re-layouts: 0.03 us -> 15.7 us
  transfers between devices with their start and end apart: 3 -> 16, of which waited for: 2 -> 8; matrix products, arithmetic and copies ran while one was open for 3% -> 2% of each run, Pallas kernels for 0% -> 20%
where the time goes in v1:
time: 171 us; the launch traced here: 169 us
  waiting for transfers between devices  62.7 us (37%)
  starting transfers between devices  43.4 us (25%)
  Pallas kernels  36.1 us (21%)
  local copies, waits for them, and re-layouts  19.8 us (12%)
  other arithmetic  6.13 us (4%)
    ppermute x6, waiting for transfers between devices, on_square(): from_left = [lax.ppermute(v, 'row', rightward) for v in from_left]  49.9 us
    pallas_call x14, Pallas kernels, shard_product(): pl.pallas_call(shard_product_kernel, grid_spec=pltpu.PrefetchScalarGridSp...  36.1 us
    ppermute x6, starting transfers between devices, on_square(): from_left = [lax.ppermute(v, 'row', rightward) for v in from_left]  28.7 us
    unnamed x42, local copies, waits for them, and re-layouts  15.7 us
    ppermute x6, starting transfers between devices, on_square(): from_right = [lax.ppermute(v, 'row', leftward) for v in from_right]  7.9 us
    ppermute x1, starting transfers between devices, on_square(): lax.ppermute(mine, ('row', 'col'), [(r * 4 + q, q * 4 + r) for r, q in pl...  5.63 us
    ppermute x1, waiting for transfers between devices, on_square(): mine = mine + lax.ppermute(sent, 'col', [(q, q ^ 2) for q in range(4)])  4.23 us
    ppermute x1, waiting for transfers between devices, on_square(): lax.ppermute(mine, ('row', 'col'), [(r * 4 + q, q * 4 + r) for r, q in pl...  3.54 us
  transfers between devices with their start and end apart: 16, of which 8 were waited for; matrix products, arithmetic and copies ran while one was open for 2% of the time, Pallas kernels for 20%

profile of v1, /device:TPU:2, one launch (start us, length us, event | category | flops | bytes accessed | tf_op | source)
XLA Modules:
  0.0 168.7 jit_solution(5754310194159689184)
XLA Ops:
  0.0 0.8 fusion.3
  0.8 1.2 slice.21
  2.1 0.7 dynamic_slice.33
  3.1 0.7 xor_select_fusion
  3.8 2.4 %compare_select_fusion = bf16[25,128,512]{2,1,0:T(8,128)(2,1)S(1)} fusion(bf16[25,128,512]{2,1,0:T(8,128)(2,1)} %param.8, s32[512]{0:T(512)} %param.10, s32[25,128]{1,0:T(8,128)S(1)} %xor_select_fusion), kind=kLoop, calls=%fused_computation | loop fusion | flops 3276800 | bytes 6568448 | tf_op jit(solution)/shard_map/jit(_where)/select_n | solution.py:23
  6.5 3.5 %collective-permute-start.9 = (bf16[15,128,256]{2,1,0:T(8,128)(2,1)S(1)}, bf16[15,128,256]{2,1,0:T(8,128)(2,1)S(1)}, u32[]{:S(2)}, u32[]{:S(2)}) collective-permute-start(bf16[15,128,256]{2,1,0:T(8,128)(2,1)S(1)} %slice.57.int_ref), channel_id=1, source_target_pairs={{0,4},{4,8},{8,12},{1,5},{5,9},{9,13},{2,6},{6,10},{10,14},{3,7},{... | collective-permute-start | bytes 2949128 | tf_op jit(solution)/shard_map/ppermute | solution.py:118
  10.0 1.3 collective-permute-start.6
  11.3 19.6 %collective-permute-done.9.int_ref = bf16[15,128,256]{2,1,0:T(8,128)(2,1)S(1)} collective-permute-done((bf16[15,128,256]{2,1,0:T(8,128)(2,1)S(1)}, bf16[15,128,256]{2,1,0:T(8,128)(2,1)S(1)}, u32[]{:S(2)}, u32[]{:S(2)}) %collective-permute-start.9) | collective-permute-done | bytes 983072 | tf_op jit(solution)/shard_map/ppermute | solution.py:118
  31.0 4.4 %collective-permute-start.10 = (bf16[15,128,256]{2,1,0:T(8,128)(2,1)S(1)}, bf16[15,128,256]{2,1,0:T(8,128)(2,1)S(1)}, u32[]{:S(2)}, u32[]{:S(2)}) collective-permute-start(bf16[15,128,256]{2,1,0:T(8,128)(2,1)S(1)} %collective-permute-done.9.int_ref), channel_id=1, source_target_pairs={{0,4},{4,8},{8,12},{1,5},{5,9},{9,13},{2,6},{6,10},{10,14},{3,7},{... | collective-permute-start | bytes 2949128 | tf_op jit(solution)/shard_map/ppermute | solution.py:118
  35.4 1.3 collective-permute-start.7
  36.7 1.0 copy-done.6
  37.8 4.6 %collective-permute-start.3 = (bf16[10,128,256]{2,1,0:T(8,128)(2,1)S(1)}, bf16[10,128,256]{2,1,0:T(8,128)(2,1)S(1)}, u32[]{:S(2)}, u32[]{:S(2)}) collective-permute-start(bf16[10,128,256]{2,1,0:T(8,128)(2,1)S(1)} %slice.56.int_ref), channel_id=1, source_target_pairs={{0,4},{4,8},{8,12},{1,5},{5,9},{9,13},{2,6},{6,10},{10,14},{3,7},{... | collective-permute-start | bytes 1966088 | tf_op jit(solution)/shard_map/ppermute | solution.py:118
  42.3 1.3 collective-permute-start
  43.6 25.9 %collective-permute-done.3.int_ref = bf16[10,128,256]{2,1,0:T(8,128)(2,1)S(1)} collective-permute-done((bf16[10,128,256]{2,1,0:T(8,128)(2,1)S(1)}, bf16[10,128,256]{2,1,0:T(8,128)(2,1)S(1)}, u32[]{:S(2)}, u32[]{:S(2)}) %collective-permute-start.3) | collective-permute-done | bytes 655392 | tf_op jit(solution)/shard_map/ppermute | solution.py:118
  69.5 5.2 %collective-permute-start.4 = (bf16[10,128,256]{2,1,0:T(8,128)(2,1)S(1)}, bf16[10,128,256]{2,1,0:T(8,128)(2,1)}, u32[]{:S(2)}, u32[]{:S(2)}) collective-permute-start(bf16[10,128,256]{2,1,0:T(8,128)(2,1)S(1)} %collective-permute-done.3.int_ref), channel_id=1, source_target_pairs={{0,4},{4,8},{8,12},{1,5},{5,9},{9,13},{2,6},{6,10},{10,14},{3,7},{... | collective-permute-start | bytes 1966088 | tf_op jit(solution)/shard_map/ppermute | solution.py:118
  74.8 0.9 copy-done.8
  75.7 1.3 collective-permute-start.1
  77.0 0.9 copy-done.10
  77.9 5.5 %collective-permute-start.11 = (bf16[15,128,256]{2,1,0:T(8,128)(2,1)S(1)}, bf16[15,128,256]{2,1,0:T(8,128)(2,1)}, u32[]{:S(2)}, u32[]{:S(2)}) collective-permute-start(bf16[15,128,256]{2,1,0:T(8,128)(2,1)S(1)} %collective-permute-done.10.int_ref), channel_id=1, source_target_pairs={{0,4},{4,8},{8,12},{1,5},{5,9},{9,13},{2,6},{6,10},{10,14},{3,7},{... | collective-permute-start | bytes 2949128 | tf_op jit(solution)/shard_map/ppermute | solution.py:118
  83.4 1.3 collective-permute-start.8
  84.7 4.4 %collective-permute-done.4.int_ref = bf16[10,128,256]{2,1,0:T(8,128)(2,1)} collective-permute-done((bf16[10,128,256]{2,1,0:T(8,128)(2,1)S(1)}, bf16[10,128,256]{2,1,0:T(8,128)(2,1)}, u32[]{:S(2)}, u32[]{:S(2)}) %collective-permute-start.4) | collective-permute-done | bytes 655392 | tf_op jit(solution)/shard_map/ppermute | solution.py:118
  89.1 5.3 %collective-permute-start.5 = (bf16[10,128,256]{2,1,0:T(8,128)(2,1)}, bf16[10,128,256]{2,1,0:T(8,128)(2,1)}, u32[]{:S(2)}, u32[]{:S(2)}) collective-permute-start(bf16[10,128,256]{2,1,0:T(8,128)(2,1)} %collective-permute-done.4.int_ref), channel_id=1, source_target_pairs={{0,4},{4,8},{8,12},{1,5},{5,9},{9,13},{2,6},{6,10},{10,14},{3,7},{... | collective-permute-start | bytes 1966088 | tf_op jit(solution)/shard_map/ppermute | solution.py:118
  94.4 0.9 collective-permute-done.1.int_ref
  95.3 1.5 collective-permute-start.2
  96.9 0.6 broadcast_xor_fusion.2
  97.9 4.7 %copy-done.1 = bf16[4,25,128,512]{3,2,1,0:T(8,128)(2,1)S(1)} copy-done((bf16[4,25,128,512]{3,2,1,0:T(8,128)(2,1)S(1)}, bf16[4,25,128,512]{3,2,1,0:T(8,128)(2,1)}, u32[]{:S(2)}) %copy-start.1) | copy-done | bytes 13107224
  102.6 2.3 %shard_map.73.total_in_ref = f32[512,256]{1,0:T(8,128)S(1)} custom-call(s32[1]{0:T(128)} %bitcast.9.block_ref, s32[15]{0:T(128)S(1)} %bitcast.40, bf16[4,25,128,512]{3,2,1,0:T(8,128)(2,1)S(1)} %copy-done.1, bf16[15,128,256]{2,1,0:T(8,128)(2,1)S(1)} %slice.57.int_ref, s32[512,1]{1,0:T(8,128)S(1)} %copy.56.left_ref, ...), custom_call_target="tpu_custom_call", output_to_operand_aliasing={{}: (6, {})} | custom-call | tf_op jit(solution)/shard_map/pallas_call | solution.py:56
  104.9 2.4 %copy-done.2 = bf16[4,25,128,512]{3,2,1,0:T(8,128)(2,1)S(1)} copy-done((bf16[4,25,128,512]{3,2,1,0:T(8,128)(2,1)S(1)}, bf16[4,25,128,512]{3,2,1,0:T(8,128)(2,1)}, u32[]{:S(2)}) %copy-start.2) | copy-done | bytes 13107224
  107.3 1.8 %shard_map.74.total_in_ref = f32[512,256]{1,0:T(8,128)S(1)} custom-call(s32[1]{0:T(128)} %bitcast.9.block_ref, s32[10]{0:T(128)S(1)} %slice.22.label_ref, bf16[4,25,128,512]{3,2,1,0:T(8,128)(2,1)S(1)} %copy-done.2, bf16[10,128,256]{2,1,0:T(8,128)(2,1)S(1)} %slice.56.int_ref, s32[512,1]{1,0:T(8,128)S(1)} %copy.56.left_ref, ...), custom_call_target="tpu_custom_call", output_to_operand_aliasing={{}: (6, {})} | custom-call | tf_op jit(solution)/shard_map/pallas_call | solution.py:56
  109.1 4.7 %copy-done.3 = bf16[4,25,128,512]{3,2,1,0:T(8,128)(2,1)S(1)} copy-done((bf16[4,25,128,512]{3,2,1,0:T(8,128)(2,1)S(1)}, bf16[4,25,128,512]{3,2,1,0:T(8,128)(2,1)}, u32[]{:S(2)}) %copy-start.3) | copy-done | bytes 13107224
  113.8 2.3 %shard_map.75.total_in_ref = f32[512,256]{1,0:T(8,128)S(1)} custom-call(s32[1]{0:T(128)} %bitcast.8.block_ref, s32[15]{0:T(128)S(1)} %bitcast.41, bf16[4,25,128,512]{3,2,1,0:T(8,128)(2,1)S(1)} %copy-done.3, bf16[15,128,256]{2,1,0:T(8,128)(2,1)S(1)} %copy-done.5, s32[512,1]{1,0:T(8,128)S(1)} %copy.56.left_ref, ...), custom_call_target="tpu_custom_call", output_to_operand_aliasing={{}: (6, {})} | custom-call | tf_op jit(solution)/shard_map/pallas_call | solution.py:56
  116.2 2.3 %shard_map.76.total_in_ref = f32[512,256]{1,0:T(8,128)S(1)} custom-call(s32[1]{0:T(128)} %bitcast.7.block_ref, s32[15]{0:T(128)S(1)} %bitcast.42, bf16[4,25,128,512]{3,2,1,0:T(8,128)(2,1)S(1)} %copy-done.3, bf16[15,128,256]{2,1,0:T(8,128)(2,1)S(1)} %copy-done.7, s32[512,1]{1,0:T(8,128)S(1)} %copy.56.left_ref, ...), custom_call_target="tpu_custom_call", output_to_operand_aliasing={{}: (6, {})} | custom-call | tf_op jit(solution)/shard_map/pallas_call | solution.py:56
  119.2 1.8 %shard_map.77.total_in_ref = f32[512,256]{1,0:T(8,128)S(1)} custom-call(s32[1]{0:T(128)} %bitcast.8.block_ref, s32[10]{0:T(128)S(1)} %slice.22.label_ref, bf16[4,25,128,512]{3,2,1,0:T(8,128)(2,1)S(1)} %bitcast.24, bf16[10,128,256]{2,1,0:T(8,128)(2,1)S(1)} %copy-done.9, s32[512,1]{1,0:T(8,128)S(1)} %copy.56.left_ref, ...), custom_call_target="tpu_custom_call", output_to_operand_aliasing={{}: (6, {})} | custom-call | tf_op jit(solution)/shard_map/pallas_call | solution.py:56
  121.0 1.8 %shard_map.78.total_in_ref = f32[512,256]{1,0:T(8,128)S(1)} custom-call(s32[1]{0:T(128)} %bitcast.7.block_ref, s32[10]{0:T(128)S(1)} %slice.22.label_ref, bf16[4,25,128,512]{3,2,1,0:T(8,128)(2,1)S(1)} %bitcast.24, bf16[10,128,256]{2,1,0:T(8,128)(2,1)S(1)} %copy-done.11, s32[512,1]{1,0:T(8,128)S(1)} %copy.56.left_ref, ...), custom_call_target="tpu_custom_call", output_to_operand_aliasing={{}: (6, {})} | custom-call | tf_op jit(solution)/shard_map/pallas_call | solution.py:56
  122.8 2.3 %shard_map.79.total_in_ref = f32[512,256]{1,0:T(8,128)S(1)} custom-call(s32[1]{0:T(128)} %bitcast.6.block_ref, s32[15]{0:T(128)S(1)} %bitcast.43, bf16[4,25,128,512]{3,2,1,0:T(8,128)(2,1)S(1)} %bitcast.24, bf16[15,128,256]{2,1,0:T(8,128)(2,1)S(1)} %collective-permute-done.10.int_ref, s32[512,1]{1,0:T(8,128)S(1)} %copy.56.left_ref, ...), custom_call_target="tpu_custom_call", output_to_operand_aliasing={{}: (6, {})} | custom-call | tf_op jit(solution)/shard_map/pallas_call | solution.py:56
  125.1 3.7 %shard_map.80.total_in_ref = f32[512,256]{1,0:T(8,128)S(1)} custom-call(s32[1]{0:T(128)} %bitcast.5.block_ref, s32[15]{0:T(128)S(1)} %bitcast.44, bf16[4,25,128,512]{3,2,1,0:T(8,128)(2,1)S(1)} %bitcast.24, bf16[15,128,256]{2,1,0:T(8,128)(2,1)} %collective-permute-done.7.int_ref, s32[512,1]{1,0:T(8,128)S(1)} %copy.56.left_ref, ...), custom_call_target="tpu_custom_call", output_to_operand_aliasing={{}: (6, {})} | custom-call | tf_op jit(solution)/shard_map/pallas_call | solution.py:56
  128.8 2.6 %shard_map.81.total_in_ref = f32[512,256]{1,0:T(8,128)S(1)} custom-call(s32[1]{0:T(128)} %bitcast.6.block_ref, s32[10]{0:T(128)S(1)} %slice.22.label_ref, bf16[4,25,128,512]{3,2,1,0:T(8,128)(2,1)S(1)} %bitcast.24, bf16[10,128,256]{2,1,0:T(8,128)(2,1)} %collective-permute-done.4.int_ref, s32[512,1]{1,0:T(8,128)S(1)} %copy.56.left_ref, ...), custom_call_target="tpu_custom_call", output_to_operand_aliasing={{}: (6, {})} | custom-call | tf_op jit(solution)/shard_map/pallas_call | solution.py:56
  131.4 2.6 %shard_map.82.total_in_ref = f32[512,256]{1,0:T(8,128)S(1)} custom-call(s32[1]{0:T(128)} %bitcast.5.block_ref, s32[10]{0:T(128)S(1)} %slice.22.label_ref, bf16[4,25,128,512]{3,2,1,0:T(8,128)(2,1)S(1)} %bitcast.24, bf16[10,128,256]{2,1,0:T(8,128)(2,1)} %collective-permute-done.1.int_ref, s32[512,1]{1,0:T(8,128)S(1)} %copy.56.left_ref, ...), custom_call_target="tpu_custom_call", output_to_operand_aliasing={{}: (6, {})} | custom-call | tf_op jit(solution)/shard_map/pallas_call | solution.py:56
  134.1 3.7 %shard_map.83.total_in_ref = f32[512,256]{1,0:T(8,128)S(1)} custom-call(s32[1]{0:T(128)} %bitcast.4.block_ref, s32[15]{0:T(128)S(1)} %bitcast.45, bf16[4,25,128,512]{3,2,1,0:T(8,128)(2,1)S(1)} %bitcast.24, bf16[15,128,256]{2,1,0:T(8,128)(2,1)} %collective-permute-done.11.int_ref, s32[512,1]{1,0:T(8,128)S(1)} %copy.56.left_ref, ...), custom_call_target="tpu_custom_call", output_to_operand_aliasing={{}: (6, {})} | custom-call | tf_op jit(solution)/shard_map/pallas_call | solution.py:56
  137.8 3.7 %shard_map.84.total_in_ref = f32[512,256]{1,0:T(8,128)S(1)} custom-call(s32[1]{0:T(128)} %bitcast.1.block_ref, s32[15]{0:T(128)S(1)} %bitcast.46, bf16[4,25,128,512]{3,2,1,0:T(8,128)(2,1)S(1)} %bitcast.24, bf16[15,128,256]{2,1,0:T(8,128)(2,1)} %collective-permute-done.8.int_ref, s32[512,1]{1,0:T(8,128)S(1)} %copy.56.left_ref, ...), custom_call_target="tpu_custom_call", output_to_operand_aliasing={{}: (6, {})} | custom-call | tf_op jit(solution)/shard_map/pallas_call | solution.py:56
  141.5 2.6 %shard_map.85.total_in_ref = f32[512,256]{1,0:T(8,128)S(1)} custom-call(s32[1]{0:T(128)} %bitcast.4.block_ref, s32[10]{0:T(128)S(1)} %slice.22.label_ref, bf16[4,25,128,512]{3,2,1,0:T(8,128)(2,1)S(1)} %bitcast.24, bf16[10,128,256]{2,1,0:T(8,128)(2,1)} %collective-permute-done.5.int_ref, s32[512,1]{1,0:T(8,128)S(1)} %copy.56.left_ref, ...), custom_call_target="tpu_custom_call", output_to_operand_aliasing={{}: (6, {})} | custom-call | tf_op jit(solution)/shard_map/pallas_call | solution.py:56
  144.2 2.6 %shard_map.86 = f32[512,256]{1,0:T(8,128)S(1)} custom-call(s32[1]{0:T(128)} %bitcast.1.block_ref, s32[10]{0:T(128)S(1)} %slice.22.label_ref, bf16[4,25,128,512]{3,2,1,0:T(8,128)(2,1)S(1)} %bitcast.24, bf16[10,128,256]{2,1,0:T(8,128)(2,1)} %collective-permute-done.2.int_ref, s32[512,1]{1,0:T(8,128)S(1)} %copy.56.left_ref, ...), custom_call_target="tpu_custom_call", output_to_operand_aliasing={{}: (6, {})} | custom-call | tf_op jit(solution)/shard_map/pallas_call | solution.py:56
  147.9 0.7 collective-permute-done.12
  150.1 4.2 %collective-permute-done.13 = f32[2,128,128]{1,0,2:T(2,128)S(1)} collective-permute-done((f32[2,128,128]{1,0,2:T(2,128)S(1)}, f32[2,128,128]{1,0,2:T(2,128)S(1)}, u32[]{:S(2)}, u32[]{:S(2)}) %collective-permute-start.13) | collective-permute-done | bytes 131104 | tf_op jit(solution)/shard_map/ppermute | solution.py:134
  155.0 5.6 %collective-permute-start.15 = (f32[2,128,128]{1,0,2:T(2,128)S(1)}, f32[2,128,128]{1,0,2:T(2,128)S(1)}, u32[]{:S(2)}, u32[]{:S(2)}) collective-permute-start(f32[2,128,128]{1,0,2:T(2,128)S(1)} %dynamic-slice_add_fusion), channel_id=1, source_target_pairs={{0,0},{1,4},{2,8},{3,12},{4,1},{5,5},{6,9},{7,13},{8,2},{9,6},{10,... | collective-permute-start | bytes 393224 | tf_op jit(solution)/shard_map/ppermute | solution.py:136
  160.7 3.4 %collective-permute-done.14 = f32[2,128,128]{1,0,2:T(2,128)S(1)} collective-permute-done((f32[2,128,128]{1,0,2:T(2,128)S(1)}, f32[2,128,128]{1,0,2:T(2,128)S(1)}, u32[]{:S(2)}, u32[]{:S(2)}) %collective-permute-start.14) | collective-permute-done | bytes 131104 | tf_op jit(solution)/shard_map/ppermute | solution.py:137
  164.1 3.5 %collective-permute-done.15 = f32[2,128,128]{1,0,2:T(2,128)S(1)} collective-permute-done((f32[2,128,128]{1,0,2:T(2,128)S(1)}, f32[2,128,128]{1,0,2:T(2,128)S(1)}, u32[]{:S(2)}, u32[]{:S(2)}) %collective-permute-start.15) | collective-permute-done | bytes 131104 | tf_op jit(solution)/shard_map/ppermute | solution.py:136
  167.7 1.0 fusion.1
  (69 shorter events, 5.0 us)
Async XLA Ops:
  0.0 2.8 %copy-start = (s32[100,8]{0,1:T(8,128)S(1)}, s32[100,8]{0,1:T(8,128)}, u32[]{:S(2)}) copy-start(s32[100,8]{0,1:T(8,128)} %param.11) | copy-start | bytes 9604
  6.2 90.7 %copy-start.14 = (s32[100]{0:T(128)S(1)}, s32[100]{0:T(128)}, u32[]{:S(2)}) copy-start(s32[100]{0:T(128)} %param.9) | copy-start | bytes 1204
  6.4 91.4 %copy-start.12 = (s32[512]{0:T(512)S(1)}, s32[512]{0:T(512)}, u32[]{:S(2)}) copy-start(s32[512]{0:T(512)} %param.10) | copy-start | bytes 6148
  6.5 24.5 %collective-permute-start.9 = (bf16[15,128,256]{2,1,0:T(8,128)(2,1)S(1)}, bf16[15,128,256]{2,1,0:T(8,128)(2,1)S(1)}, u32[]{:S(2)}, u32[]{:S(2)}) collective-permute-start(bf16[15,128,256]{2,1,0:T(8,128)(2,1)S(1)} %slice.57.int_ref), channel_id=1, source_target_pairs={{0,4},{4,8},{8,12},{1,5},{5,9},{9,13},{2,6},{6,10},{10,14},{3,7},{... | collective-permute-start | bytes 2949128 | tf_op jit(solution)/shard_map/ppermute | solution.py:118
  10.0 25.4 %collective-permute-start.6 = (bf16[15,128,256]{2,1,0:T(8,128)(2,1)S(1)}, bf16[15,128,256]{2,1,0:T(8,128)(2,1)S(1)}, u32[]{:S(2)}, u32[]{:S(2)}) collective-permute-start(bf16[15,128,256]{2,1,0:T(8,128)(2,1)S(1)} %slice.57.int_ref), channel_id=1, source_target_pairs={{4,0},{8,4},{12,8},{5,1},{9,5},{13,9},{6,2},{10,6},{14,10},{7,3},{... | collective-permute-start | bytes 2949128 | tf_op jit(solution)/shard_map/ppermute | solution.py:119
  31.0 46.9 %copy-start.4 = (bf16[15,128,256]{2,1,0:T(8,128)(2,1)}, bf16[15,128,256]{2,1,0:T(8,128)(2,1)S(1)}, u32[]{:S(2)}) copy-start(bf16[15,128,256]{2,1,0:T(8,128)(2,1)S(1)} %collective-permute-done.9.int_ref) | copy-start | bytes 2949124
  31.0 46.9 %collective-permute-start.10 = (bf16[15,128,256]{2,1,0:T(8,128)(2,1)S(1)}, bf16[15,128,256]{2,1,0:T(8,128)(2,1)S(1)}, u32[]{:S(2)}, u32[]{:S(2)}) collective-permute-start(bf16[15,128,256]{2,1,0:T(8,128)(2,1)S(1)} %collective-permute-done.9.int_ref), channel_id=1, source_target_pairs={{0,4},{4,8},{8,12},{1,5},{5,9},{9,13},{2,6},{6,10},{10,14},{3,7},{... | collective-permute-start | bytes 2949128 | tf_op jit(solution)/shard_map/ppermute | solution.py:118
  35.4 48.0 %collective-permute-start.7 = (bf16[15,128,256]{2,1,0:T(8,128)(2,1)S(1)}, bf16[15,128,256]{2,1,0:T(8,128)(2,1)}, u32[]{:S(2)}, u32[]{:S(2)}) collective-permute-start(bf16[15,128,256]{2,1,0:T(8,128)(2,1)S(1)} %collective-permute-done.6.int_ref), channel_id=1, source_target_pairs={{4,0},{8,4},{12,8},{5,1},{9,5},{13,9},{6,2},{10,6},{14,10},{7,3},{... | collective-permute-start | bytes 2949128 | tf_op jit(solution)/shard_map/ppermute | solution.py:119
  36.7 1.0 copy-start.6
  37.8 31.8 %collective-permute-start.3 = (bf16[10,128,256]{2,1,0:T(8,128)(2,1)S(1)}, bf16[10,128,256]{2,1,0:T(8,128)(2,1)S(1)}, u32[]{:S(2)}, u32[]{:S(2)}) collective-permute-start(bf16[10,128,256]{2,1,0:T(8,128)(2,1)S(1)} %slice.56.int_ref), channel_id=1, source_target_pairs={{0,4},{4,8},{8,12},{1,5},{5,9},{9,13},{2,6},{6,10},{10,14},{3,7},{... | collective-permute-start | bytes 1966088 | tf_op jit(solution)/shard_map/ppermute | solution.py:118
  42.3 33.3 %collective-permute-start = (bf16[10,128,256]{2,1,0:T(8,128)(2,1)S(1)}, bf16[10,128,256]{2,1,0:T(8,128)(2,1)S(1)}, u32[]{:S(2)}, u32[]{:S(2)}) collective-permute-start(bf16[10,128,256]{2,1,0:T(8,128)(2,1)S(1)} %slice.56.int_ref), channel_id=1, source_target_pairs={{4,0},{8,4},{12,8},{5,1},{9,5},{13,9},{6,2},{10,6},{14,10},{7,3},{... | collective-permute-start | bytes 1966088 | tf_op jit(solution)/shard_map/ppermute | solution.py:119
  69.5 19.6 %collective-permute-start.4 = (bf16[10,128,256]{2,1,0:T(8,128)(2,1)S(1)}, bf16[10,128,256]{2,1,0:T(8,128)(2,1)}, u32[]{:S(2)}, u32[]{:S(2)}) collective-permute-start(bf16[10,128,256]{2,1,0:T(8,128)(2,1)S(1)} %collective-permute-done.3.int_ref), channel_id=1, source_target_pairs={{0,4},{4,8},{8,12},{1,5},{5,9},{9,13},{2,6},{6,10},{10,14},{3,7},{... | collective-permute-start | bytes 1966088 | tf_op jit(solution)/shard_map/ppermute | solution.py:118
  74.8 0.9 copy-start.8
  75.7 19.7 %collective-permute-start.1 = (bf16[10,128,256]{2,1,0:T(8,128)(2,1)S(1)}, bf16[10,128,256]{2,1,0:T(8,128)(2,1)}, u32[]{:S(2)}, u32[]{:S(2)}) collective-permute-start(bf16[10,128,256]{2,1,0:T(8,128)(2,1)S(1)} %collective-permute-done.int_ref), channel_id=1, source_target_pairs={{4,0},{8,4},{12,8},{5,1},{9,5},{13,9},{6,2},{10,6},{14,10},{7,3},{... | collective-permute-start | bytes 1966088 | tf_op jit(solution)/shard_map/ppermute | solution.py:119
  77.0 0.9 copy-start.10
  77.9 56.2 %collective-permute-start.11 = (bf16[15,128,256]{2,1,0:T(8,128)(2,1)S(1)}, bf16[15,128,256]{2,1,0:T(8,128)(2,1)}, u32[]{:S(2)}, u32[]{:S(2)}) collective-permute-start(bf16[15,128,256]{2,1,0:T(8,128)(2,1)S(1)} %collective-permute-done.10.int_ref), channel_id=1, source_target_pairs={{0,4},{4,8},{8,12},{1,5},{5,9},{9,13},{2,6},{6,10},{10,14},{3,7},{... | collective-permute-start | bytes 2949128 | tf_op jit(solution)/shard_map/ppermute | solution.py:118
  83.4 54.4 %collective-permute-start.8 = (bf16[15,128,256]{2,1,0:T(8,128)(2,1)}, bf16[15,128,256]{2,1,0:T(8,128)(2,1)}, u32[]{:S(2)}, u32[]{:S(2)}) collective-permute-start(bf16[15,128,256]{2,1,0:T(8,128)(2,1)} %collective-permute-done.7.int_ref), channel_id=1, source_target_pairs={{4,0},{8,4},{12,8},{5,1},{9,5},{13,9},{6,2},{10,6},{14,10},{7,3},{... | collective-permute-start | bytes 2949128 | tf_op jit(solution)/shard_map/ppermute | solution.py:119
  89.1 52.4 %collective-permute-start.5 = (bf16[10,128,256]{2,1,0:T(8,128)(2,1)}, bf16[10,128,256]{2,1,0:T(8,128)(2,1)}, u32[]{:S(2)}, u32[]{:S(2)}) collective-permute-start(bf16[10,128,256]{2,1,0:T(8,128)(2,1)} %collective-permute-done.4.int_ref), channel_id=1, source_target_pairs={{0,4},{4,8},{8,12},{1,5},{5,9},{9,13},{2,6},{6,10},{10,14},{3,7},{... | collective-permute-start | bytes 1966088 | tf_op jit(solution)/shard_map/ppermute | solution.py:118
  95.3 48.8 %collective-permute-start.2 = (bf16[10,128,256]{2,1,0:T(8,128)(2,1)}, bf16[10,128,256]{2,1,0:T(8,128)(2,1)}, u32[]{:S(2)}, u32[]{:S(2)}) collective-permute-start(bf16[10,128,256]{2,1,0:T(8,128)(2,1)} %collective-permute-done.1.int_ref), channel_id=1, source_target_pairs={{4,0},{8,4},{12,8},{5,1},{9,5},{13,9},{6,2},{10,6},{14,10},{7,3},{... | collective-permute-start | bytes 1966088 | tf_op jit(solution)/shard_map/ppermute | solution.py:119
  97.8 4.7 %copy-start.1 = (bf16[4,25,128,512]{3,2,1,0:T(8,128)(2,1)S(1)}, bf16[4,25,128,512]{3,2,1,0:T(8,128)(2,1)}, u32[]{:S(2)}) copy-start(bf16[4,25,128,512]{3,2,1,0:T(8,128)(2,1)} %amp_ref.27) | copy-start | bytes 39321604
  102.6 4.7 %copy-start.2 = (bf16[4,25,128,512]{3,2,1,0:T(8,128)(2,1)S(1)}, bf16[4,25,128,512]{3,2,1,0:T(8,128)(2,1)}, u32[]{:S(2)}) copy-start(bf16[4,25,128,512]{3,2,1,0:T(8,128)(2,1)} %amp_ref.27) | copy-start | bytes 39321604
  107.3 1.8 %copy-start.5 = (bf16[15,128,256]{2,1,0:T(8,128)(2,1)S(1)}, bf16[15,128,256]{2,1,0:T(8,128)(2,1)}, u32[]{:S(2)}) copy-start(bf16[15,128,256]{2,1,0:T(8,128)(2,1)} %copy-done.4) | copy-start | bytes 2949124
  109.1 4.7 %copy-start.3 = (bf16[4,25,128,512]{3,2,1,0:T(8,128)(2,1)S(1)}, bf16[4,25,128,512]{3,2,1,0:T(8,128)(2,1)}, u32[]{:S(2)}) copy-start(bf16[4,25,128,512]{3,2,1,0:T(8,128)(2,1)} %amp_ref.27) | copy-start | bytes 39321604
  113.8 2.3 %copy-start.7 = (bf16[15,128,256]{2,1,0:T(8,128)(2,1)S(1)}, bf16[15,128,256]{2,1,0:T(8,128)(2,1)}, u32[]{:S(2)}) copy-start(bf16[15,128,256]{2,1,0:T(8,128)(2,1)} %copy-done.6) | copy-start | bytes 2949124
  113.8 4.6 %slice-start = ((s8[13107200]{0:T(1024)(128)(4,1)}), s8[4194304]{0:T(1024)(128)(4,1)S(1)}, s32[]{:S(2)}) async-start(s8[13107200]{0:T(1024)(128)(4,1)} %bitcast.23), calls=%async_computation | async-start | bytes 8388608
  113.8 4.6 %slice-start.1 = ((s8[13107200]{0:T(1024)(128)(4,1)}), s8[4194304]{0:T(1024)(128)(4,1)S(1)}, s32[]{:S(2)}) async-start(s8[13107200]{0:T(1024)(128)(4,1)} %bitcast.23), calls=%async_computation.1 | async-start | bytes 8388608
  116.1 2.9 %slice-start.2 = ((s8[13107200]{0:T(1024)(128)(4,1)}), s8[4194304]{0:T(1024)(128)(4,1)S(1)}, s32[]{:S(2)}) async-start(s8[13107200]{0:T(1024)(128)(4,1)} %bitcast.23), calls=%async_computation.2 | async-start | bytes 8388608
  116.2 2.9 %slice-start.3 = ((s8[13107200]{0:T(1024)(128)(4,1)}), s8[524288]{0:T(1024)(128)(4,1)S(1)}, s32[]{:S(2)}) async-start(s8[13107200]{0:T(1024)(128)(4,1)} %bitcast.23), calls=%async_computation.3 | async-start | bytes 1048576
  116.2 3.0 %copy-start.9 = (bf16[10,128,256]{2,1,0:T(8,128)(2,1)S(1)}, bf16[10,128,256]{2,1,0:T(8,128)(2,1)}, u32[]{:S(2)}) copy-start(bf16[10,128,256]{2,1,0:T(8,128)(2,1)} %copy-done.8) | copy-start | bytes 1966084
  119.2 1.8 %copy-start.11 = (bf16[10,128,256]{2,1,0:T(8,128)(2,1)S(1)}, bf16[10,128,256]{2,1,0:T(8,128)(2,1)}, u32[]{:S(2)}) copy-start(bf16[10,128,256]{2,1,0:T(8,128)(2,1)} %copy-done.10) | copy-start | bytes 1966084
  144.1 3.0 %copy-start.15 = (f32[100]{0:T(128)S(1)}, f32[100]{0:T(128)}, u32[]{:S(2)}) copy-start(f32[100]{0:T(128)} %param.12) | copy-start | bytes 1204
  144.1 5.9 %copy-start.13 = (f32[512]{0:T(512)S(1)}, f32[512]{0:T(512)}, u32[]{:S(2)}) copy-start(f32[512]{0:T(512)} %param.13) | copy-start | bytes 6148
  147.0 1.6 collective-permute-start.12
  148.8 5.6 %collective-permute-start.13 = (f32[2,128,128]{1,0,2:T(2,128)S(1)}, f32[2,128,128]{1,0,2:T(2,128)S(1)}, u32[]{:S(2)}, u32[]{:S(2)}) collective-permute-start(f32[2,128,128]{1,0,2:T(2,128)S(1)} %constant_dynamic-slice_fusion), channel_id=1, source_target_pairs={{0,2},{1,3},{2,0},{3,1},{4,6},{5,7},{6,4},{7,5},{8,10},{9,11},{10,... | collective-permute-start | bytes 393224 | tf_op jit(solution)/shard_map/ppermute | solution.py:134
  154.4 9.7 %collective-permute-start.14 = (f32[2,128,128]{1,0,2:T(2,128)S(1)}, f32[2,128,128]{1,0,2:T(2,128)S(1)}, u32[]{:S(2)}, u32[]{:S(2)}) collective-permute-start(f32[2,128,128]{1,0,2:T(2,128)S(1)} %dynamic-slice_add_fusion), channel_id=1, source_target_pairs={{0,8},{1,12},{2,0},{3,4},{4,9},{5,13},{6,1},{7,5},{8,10},{9,14},{1... | collective-permute-start | bytes 393224 | tf_op jit(solution)/shard_map/ppermute | solution.py:137
  155.0 12.6 %collective-permute-start.15 = (f32[2,128,128]{1,0,2:T(2,128)S(1)}, f32[2,128,128]{1,0,2:T(2,128)S(1)}, u32[]{:S(2)}, u32[]{:S(2)}) collective-permute-start(f32[2,128,128]{1,0,2:T(2,128)S(1)} %dynamic-slice_add_fusion), channel_id=1, source_target_pairs={{0,0},{1,4},{2,8},{3,12},{4,1},{5,5},{6,9},{7,13},{8,2},{9,6},{10,... | collective-permute-start | bytes 393224 | tf_op jit(solution)/shard_map/ppermute | solution.py:136

commit v2 on v1

--- a/solution.py
+++ b/solution.py
@@ -24,54 +24,77 @@
     return kept[:, :, :FOLD] + kept[:, :, FOLD:]
 
 
-def shard_product_kernel(
-    block_ref, label_ref, amp_ref, int_ref, left_ref, right_ref, total_in_ref, total_ref, mix_ref
-):
+def shard_product_kernel(block_ref, valid_ref, label_ref, amp_ref, *refs):
+    sides = len(refs) - 5
+    int_refs = refs[:sides]
+    left_ref, right_ref, total_in_ref, total_ref, mix_ref = refs[sides:]
     step = pl.program_id(0)
+    steps = pl.num_programs(0) // sides
+    k_step = amp_ref.shape[1]
+    rows = amp_ref.shape[0] * amp_ref.shape[2]
 
     @pl.when(step == 0)
     def _():
         total_ref[...] = total_in_ref[...]
-        mixed = jnp.bitwise_xor(left_ref[...], right_ref[...])
-        mix_ref[...] = mixed.astype(jnp.float32).astype(jnp.bfloat16)
-
-    rows = amp_ref.shape[0] * amp_ref.shape[2]
-    mixed = mix_ref[...]
-    pieces = []
-    for j in range(amp_ref.shape[1]):
-        label = label_ref[step * amp_ref.shape[1] + j].astype(jnp.float32)
-        tile = amp_ref[:, j].reshape(rows, amp_ref.shape[3])
-        wanted = jnp.full(mixed.shape, label, jnp.float32).astype(jnp.bfloat16)
-        pieces.append(jnp.where(mixed == wanted, tile, jnp.zeros_like(tile)))
-    lhs = jnp.concatenate(pieces, axis=1)
-    rhs = int_ref[...].reshape(-1, int_ref.shape[2])
-    total_ref[...] += jnp.dot(lhs, rhs, preferred_element_type=jnp.float32)
-
-
-def shard_product(total, amplitudes, fold, block, labels, k_start, row_labels, col_labels):
+
+    for side in range(sides):
+        local = step - side * steps
+
+        @pl.when((local == 0) & (valid_ref[side] == 1))
+        def _():
+            mixed = jnp.bitwise_xor(left_ref[...], right_ref[...])
+            mix_ref[...] = mixed.astype(jnp.float32).astype(jnp.bfloat16)
+
+        @pl.when((local >= 0) & (local < steps) & (valid_ref[side] == 1))
+        def _(local=local, int_ref=int_refs[side]):
+            mixed = mix_ref[...]
+            pieces = []
+            for j in range(k_step):
+                label = label_ref[local * k_step + j].astype(jnp.float32)
+                tile = amp_ref[:, j].reshape(rows, amp_ref.shape[3])
+                wanted = jnp.full(mixed.shape, label, jnp.float32).astype(jnp.bfloat16)
+                pieces.append(jnp.where(mixed == wanted, tile, jnp.zeros_like(tile)))
+            lhs = jnp.concatenate(pieces, axis=1)
+            rhs = int_ref[...].reshape(-1, int_ref.shape[2])
+            total_ref[...] += jnp.dot(lhs, rhs, preferred_element_type=jnp.float32)
+
+
+def shard_product(total, amplitudes, folds, sources, source_count, labels, k_start, row_labels, col_labels):
     batch, _, share, _ = amplitudes.shape
-    k_count, depth, width = fold.shape
+    k_count, depth, width = folds[0].shape
     first = k_start // K_STEP
     rows = batch * share
+    steps = k_count // K_STEP
+    sides = len(folds)
+    sources = jnp.stack(sources).astype(jnp.int32)
+    valid = ((sources >= 0) & (sources < source_count)).astype(jnp.int32)
+    blocks = jnp.clip(sources, 0, source_count - 1)
+
+    def amp_map(g, s, v, l):
+        return (0, first + g % steps, 0, s[g // steps])
+
+    def int_map(side):
+        return lambda g, s, v, l: (jnp.clip(g - side * steps, 0, steps - 1), 0, 0)
+
     return pl.pallas_call(
         shard_product_kernel,
         grid_spec=pltpu.PrefetchScalarGridSpec(
-            num_scalar_prefetch=2,
-            grid=(k_count // K_STEP,),
-            in_specs=[
-                pl.BlockSpec((batch, K_STEP, share, depth), lambda k, s, l: (0, first + k, 0, s[0])),
-                pl.BlockSpec((K_STEP, depth, width), lambda k, s, l: (k, 0, 0)),
-                pl.BlockSpec((rows, 1), lambda k, s, l: (0, 0)),
-                pl.BlockSpec((1, depth), lambda k, s, l: (0, s[0])),
-                pl.BlockSpec((rows, width), lambda k, s, l: (0, 0)),
+            num_scalar_prefetch=3,
+            grid=(sides * steps,),
+            in_specs=[pl.BlockSpec((batch, K_STEP, share, depth), amp_map)]
+            + [pl.BlockSpec((K_STEP, depth, width), int_map(side)) for side in range(sides)]
+            + [
+                pl.BlockSpec((rows, 1), lambda g, s, v, l: (0, 0)),
+                pl.BlockSpec((1, depth), lambda g, s, v, l: (0, s[g // steps])),
+                pl.BlockSpec((rows, width), lambda g, s, v, l: (0, 0)),
             ],
-            out_specs=pl.BlockSpec((rows, width), lambda k, s, l: (0, 0)),
+            out_specs=pl.BlockSpec((rows, width), lambda g, s, v, l: (0, 0)),
             scratch_shapes=[pltpu.VMEM((rows, depth), jnp.bfloat16)],
         ),
         out_shape=jax.ShapeDtypeStruct((rows, width), jnp.float32),
-        input_output_aliases={6: 0},
+        input_output_aliases={6 + sides: 0},
         compiler_params=pltpu.CompilerParams(vmem_limit_bytes=32 * 1024 * 1024),
-    )(block, labels, amplitudes, fold, row_labels, col_labels, total)
+    )(blocks, valid, labels, amplitudes, *folds, row_labels, col_labels, total)
 
 
 def finish(cycle, occ_irrep, vir_irrep, occ_energy, vir_energy, a_start, a_size, b_start, b_size, batch):
@@ -103,24 +126,26 @@
     chunks = [(0, 15), (15, occ_share)]
     total = jnp.zeros((batch * share, FOLD), jnp.float32)
 
-    def add(total, part, source, chunk):
-        block = jnp.clip(source, 0, rows_n - 1).astype(jnp.int32).reshape(1)
+    def add(total, parts, sources, chunk):
         return shard_product(
-            total, amplitudes, part, block, occ_local[chunk[0]:chunk[1]], chunk[0], row_labels, col_labels
+            total, amplitudes, parts, sources, rows_n, occ_local[chunk[0]:chunk[1]], chunk[0],
+            row_labels, col_labels,
         )
 
     own = [fold[lo:hi] for lo, hi in chunks]
     rightward = [(i, i + 1) for i in range(rows_n - 1)]
     leftward = [(i + 1, i) for i in range(rows_n - 1)]
-    from_left, from_right = own, own
-    for distance in range(rows_n):
-        if distance:
-            from_left = [lax.ppermute(v, "row", rightward) for v in from_left]
-            from_right = [lax.ppermute(v, "row", leftward) for v in from_right]
+    held = [((v, v), (v,), (row,)) for v in own]
+    for distance in range(1, rows_n + 1):
         for n, chunk in enumerate(chunks):
-            total = add(total, from_left[n], row - distance, chunk)
-            if distance:
-                total = add(total, from_right[n], row + distance, chunk)
+            (left, right), parts, sources = held[n]
+            if distance < rows_n:
+                left = lax.ppermute(left, "row", rightward)
+                right = lax.ppermute(right, "row", leftward)
+            total = add(total, parts, sources, chunk)
+            if distance < rows_n:
+                left, right, _ = lax.optimization_barrier((left, right, total))
+            held[n] = ((left, right), (left, right), (row - distance, row + distance))
     half = col % 2
     chip = col // 2
     width = FOLD // 2

time: 171 us -> 156 us (0.912)
  waiting for transfers between devices: 62.7 us -> 48.8 us
  local copies, waits for them, and re-layouts: 19.8 us -> 32.8 us
  starting transfers between devices: 43.4 us -> 35.9 us
  Pallas kernels: 36.1 us -> 29.5 us
    ppermute x12, waiting for transfers between devices: 50.8 us -> 37.3 us  [the longest x6 27.1 us: on_square(): right = lax.ppermute(right, 'row', leftward)]
    unnamed x42 -> x28, local copies, waits for them, and re-layouts: 15.7 us -> 28.7 us
    pallas_call x14 -> x8, Pallas kernels: 36.1 us -> 29.5 us  [shard_product(): pl.pallas_call(shard_product_kernel, grid_spec=pltpu.PrefetchScalarGridSp...]
    ppermute x12, starting transfers between devices: 36.6 us -> 31.5 us  [the longest x6 23.8 us: on_square(): left = lax.ppermute(left, 'row', rightward)]
    ppermute x1, starting transfers between devices: 5.63 us -> 3.17 us  [on_square(): lax.ppermute(mine, ('row', 'col'), [(r * 4 + q, q * 4 + r) for r, q in pl...]
  transfers between devices with their start and end apart: 16 -> 16, of which waited for: 8 -> 14; matrix products, arithmetic and copies ran while one was open for 2% -> 2% of each run, Pallas kernels for 20% -> 13%
where the time goes in v2:
time: 156 us; the launch traced here: 154 us
  waiting for transfers between devices  48.8 us (31%)
  starting transfers between devices  35.9 us (23%)
  local copies, waits for them, and re-layouts  32.8 us (21%)
  Pallas kernels  29.5 us (19%)
  other arithmetic  6.6 us (4%)
    pallas_call x8, Pallas kernels, shard_product(): pl.pallas_call(shard_product_kernel, grid_spec=pltpu.PrefetchScalarGridSp...  29.5 us
    unnamed x28, local copies, waits for them, and re-layouts  28.7 us
    ppermute x6, waiting for transfers between devices, on_square(): right = lax.ppermute(right, 'row', leftward)  27.1 us
    ppermute x6, starting transfers between devices, on_square(): left = lax.ppermute(left, 'row', rightward)  23.8 us
    ppermute x6, waiting for transfers between devices, on_square(): left = lax.ppermute(left, 'row', rightward)  10.2 us
    ppermute x6, starting transfers between devices, on_square(): right = lax.ppermute(right, 'row', leftward)  7.7 us
    ppermute x1, waiting for transfers between devices, on_square(): mine = mine + lax.ppermute(sent, 'col', [(q, q ^ 2) for q in range(4)])  4.23 us
    ppermute x1, waiting for transfers between devices, on_square(): lax.ppermute(mine, ('row', 'col'), [(r * 4 + q, (q ^ 2) * 4 + r) for r, q...  3.4 us
  transfers between devices with their start and end apart: 16, of which 14 were waited for; matrix products, arithmetic and copies ran while one was open for 2% of the time, Pallas kernels for 13%

profile of v2, /device:TPU:2, one launch (start us, length us, event | category | flops | bytes accessed | tf_op | source)
XLA Modules:
  0.0 154.0 jit_solution(873081432210046187)
XLA Ops:
  0.0 0.8 fusion.3
  0.8 1.2 slice.39
  2.1 0.7 dynamic_slice.33
  3.1 0.7 xor_select_fusion
  3.8 2.4 %compare_select_fusion = bf16[25,128,512]{2,1,0:T(8,128)(2,1)S(1)} fusion(bf16[25,128,512]{2,1,0:T(8,128)(2,1)} %param.8, s32[512]{0:T(512)} %param.10, s32[25,128]{1,0:T(8,128)S(1)} %xor_select_fusion), kind=kLoop, calls=%fused_computation | loop fusion | flops 3276800 | bytes 6568448 | tf_op jit(solution)/shard_map/jit(_where)/select_n | solution.py:23
  6.5 4.5 %collective-permute-start.4 = (bf16[15,128,256]{2,1,0:T(8,128)(2,1)S(1)}, bf16[15,128,256]{2,1,0:T(8,128)(2,1)}, u32[]{:S(2)}, u32[]{:S(2)}) collective-permute-start(bf16[15,128,256]{2,1,0:T(8,128)(2,1)S(1)} %slice.51.refs_0_), channel_id=1, source_target_pairs={{0,4},{4,8},{8,12},{1,5},{5,9},{9,13},{2,6},{6,10},{10,14},{3,7},{... | collective-permute-start | bytes 2949128 | tf_op jit(solution)/shard_map/ppermute | solution.py:143
  11.0 1.3 collective-permute-start.5
  12.3 5.4 %collective-permute-start = (bf16[10,128,256]{2,1,0:T(8,128)(2,1)S(1)}, bf16[10,128,256]{2,1,0:T(8,128)(2,1)}, u32[]{:S(2)}, u32[]{:S(2)}) collective-permute-start(bf16[10,128,256]{2,1,0:T(8,128)(2,1)S(1)} %slice.50.refs_0_), channel_id=1, source_target_pairs={{0,4},{4,8},{8,12},{1,5},{5,9},{9,13},{2,6},{6,10},{10,14},{3,7},{... | collective-permute-start | bytes 1966088 | tf_op jit(solution)/shard_map/ppermute | solution.py:143
  17.7 1.3 collective-permute-start.1
  19.0 0.7 broadcast_xor_fusion.2
  19.9 4.7 %copy-done.1 = bf16[4,25,128,512]{3,2,1,0:T(8,128)(2,1)S(1)} copy-done((bf16[4,25,128,512]{3,2,1,0:T(8,128)(2,1)S(1)}, bf16[4,25,128,512]{3,2,1,0:T(8,128)(2,1)}, u32[]{:S(2)}) %copy-start.1) | copy-done | bytes 13107224
  24.6 2.4 %shard_map.73.refs_3_ = f32[512,256]{1,0:T(8,128)S(1)} custom-call(s32[1]{0:T(128)} %bitcast.3.block_ref, s32[1]{0:T(128)} %bitcast.4.valid_ref, s32[15]{0:T(128)S(1)} %bitcast.33, bf16[4,25,128,512]{3,2,1,0:T(8,128)(2,1)S(1)} %copy-done.1, bf16[15,128,256]{2,1,0:T(8,128)(2,1)S(1)} %slice.51.refs_0_, ...), custom_call_target="tpu_custom_call", output_to_operand_aliasing={{}: (7, {})} | custom-call | tf_op jit(solution)/shard_map/pallas_call | solution.py:79
  27.1 5.0 %collective-permute-done.4.refs_0_ = bf16[15,128,256]{2,1,0:T(8,128)(2,1)} collective-permute-done((bf16[15,128,256]{2,1,0:T(8,128)(2,1)S(1)}, bf16[15,128,256]{2,1,0:T(8,128)(2,1)}, u32[]{:S(2)}, u32[]{:S(2)}) %collective-permute-start.4) | collective-permute-done | bytes 983072 | tf_op jit(solution)/shard_map/ppermute | solution.py:143
  32.1 5.5 %collective-permute-done.5.refs_1_ = bf16[15,128,256]{2,1,0:T(8,128)(2,1)} collective-permute-done((bf16[15,128,256]{2,1,0:T(8,128)(2,1)S(1)}, bf16[15,128,256]{2,1,0:T(8,128)(2,1)}, u32[]{:S(2)}, u32[]{:S(2)}) %collective-permute-start.5) | collective-permute-done | bytes 983072 | tf_op jit(solution)/shard_map/ppermute | solution.py:144
  37.6 2.6 %collective-permute-start.8 = (bf16[15,128,256]{2,1,0:T(8,128)(2,1)}, bf16[15,128,256]{2,1,0:T(8,128)(2,1)S(1)}, u32[]{:S(2)}, u32[]{:S(2)}) collective-permute-start(bf16[15,128,256]{2,1,0:T(8,128)(2,1)} %collective-permute-done.4.refs_0_), channel_id=1, source_target_pairs={{0,4},{4,8},{8,12},{1,5},{5,9},{9,13},{2,6},{6,10},{10,14},{3,7},{... | collective-permute-start | bytes 2949128 | tf_op jit(solution)/shard_map/ppermute | solution.py:143
  40.2 1.3 collective-permute-start.9
  41.6 1.9 %shard_map.74.refs_4_ = f32[512,256]{1,0:T(8,128)S(1)} custom-call(s32[1]{0:T(128)} %bitcast.3.block_ref, s32[1]{0:T(128)} %bitcast.4.valid_ref, s32[10]{0:T(128)S(1)} %slice.40.label_ref, bf16[4,25,128,512]{3,2,1,0:T(8,128)(2,1)S(1)} %copy-done.2, bf16[10,128,256]{2,1,0:T(8,128)(2,1)S(1)} %slice.50.refs_0_, ...), custom_call_target="tpu_custom_call", output_to_operand_aliasing={{}: (7, {})} | custom-call | tf_op jit(solution)/shard_map/pallas_call | solution.py:79
  43.5 2.7 %collective-permute-done.refs_0_ = bf16[10,128,256]{2,1,0:T(8,128)(2,1)} collective-permute-done((bf16[10,128,256]{2,1,0:T(8,128)(2,1)S(1)}, bf16[10,128,256]{2,1,0:T(8,128)(2,1)}, u32[]{:S(2)}, u32[]{:S(2)}) %collective-permute-start) | collective-permute-done | bytes 655392 | tf_op jit(solution)/shard_map/ppermute | solution.py:143
  46.2 5.5 %collective-permute-done.1.refs_1_ = bf16[10,128,256]{2,1,0:T(8,128)(2,1)} collective-permute-done((bf16[10,128,256]{2,1,0:T(8,128)(2,1)S(1)}, bf16[10,128,256]{2,1,0:T(8,128)(2,1)}, u32[]{:S(2)}, u32[]{:S(2)}) %collective-permute-start.1) | collective-permute-done | bytes 655392 | tf_op jit(solution)/shard_map/ppermute | solution.py:144
  51.7 2.6 %collective-permute-start.2 = (bf16[10,128,256]{2,1,0:T(8,128)(2,1)}, bf16[10,128,256]{2,1,0:T(8,128)(2,1)S(1)}, u32[]{:S(2)}, u32[]{:S(2)}) collective-permute-start(bf16[10,128,256]{2,1,0:T(8,128)(2,1)} %collective-permute-done.refs_0_), channel_id=1, source_target_pairs={{0,4},{4,8},{8,12},{1,5},{5,9},{9,13},{2,6},{6,10},{10,14},{3,7},{... | collective-permute-start | bytes 1966088 | tf_op jit(solution)/shard_map/ppermute | solution.py:143
  54.2 1.3 collective-permute-start.3
  55.7 4.7 %copy-done.3 = bf16[4,25,128,512]{3,2,1,0:T(8,128)(2,1)S(1)} copy-done((bf16[4,25,128,512]{3,2,1,0:T(8,128)(2,1)S(1)}, bf16[4,25,128,512]{3,2,1,0:T(8,128)(2,1)}, u32[]{:S(2)}) %copy-start.3) | copy-done | bytes 13107224
  60.4 5.3 %shard_map.75.refs_4_ = f32[512,256]{1,0:T(8,128)S(1)} custom-call(s32[2]{0:T(128)S(1)} %broadcast_clamp_fusion.1.block_ref, s32[2]{0:T(128)S(1)} %and_convert_fusion.1.valid_ref, s32[15]{0:T(128)S(1)} %bitcast.34, bf16[4,25,128,512]{3,2,1,0:T(8,128)(2,1)S(1)} %copy-done.3, ...), custom_call_target="tpu_custom_call", output_to_operand_aliasing={{}: (8, {})} | custom-call | tf_op jit(solution)/shard_map/pallas_call | solution.py:79
  65.7 1.7 %collective-permute-done.8.refs_0_ = bf16[15,128,256]{2,1,0:T(8,128)(2,1)S(1)} collective-permute-done((bf16[15,128,256]{2,1,0:T(8,128)(2,1)}, bf16[15,128,256]{2,1,0:T(8,128)(2,1)S(1)}, u32[]{:S(2)}, u32[]{:S(2)}) %collective-permute-start.8) | collective-permute-done | bytes 983072 | tf_op jit(solution)/shard_map/ppermute | solution.py:143
  67.3 5.3 %collective-permute-done.9.refs_1_ = bf16[15,128,256]{2,1,0:T(8,128)(2,1)S(1)} collective-permute-done((bf16[15,128,256]{2,1,0:T(8,128)(2,1)}, bf16[15,128,256]{2,1,0:T(8,128)(2,1)S(1)}, u32[]{:S(2)}, u32[]{:S(2)}) %collective-permute-start.9) | collective-permute-done | bytes 983072 | tf_op jit(solution)/shard_map/ppermute | solution.py:144
  72.6 3.5 %collective-permute-start.10 = (bf16[15,128,256]{2,1,0:T(8,128)(2,1)S(1)}, bf16[15,128,256]{2,1,0:T(8,128)(2,1)}, u32[]{:S(2)}, u32[]{:S(2)}) collective-permute-start(bf16[15,128,256]{2,1,0:T(8,128)(2,1)S(1)} %collective-permute-done.8.refs_0_), channel_id=1, source_target_pairs={{0,4},{4,8},{8,12},{1,5},{5,9},{9,13},{2,6},{6,10},{10,14},{3,7},{... | collective-permute-start | bytes 2949128 | tf_op jit(solution)/shard_map/ppermute | solution.py:143
  76.1 1.3 collective-permute-start.11
  77.4 4.7 %copy-done.4 = bf16[4,25,128,512]{3,2,1,0:T(8,128)(2,1)S(1)} copy-done((bf16[4,25,128,512]{3,2,1,0:T(8,128)(2,1)S(1)}, bf16[4,25,128,512]{3,2,1,0:T(8,128)(2,1)}, u32[]{:S(2)}) %copy-start.4) | copy-done | bytes 13107224
  82.1 3.6 %shard_map.76.refs_4_ = f32[512,256]{1,0:T(8,128)S(1)} custom-call(s32[2]{0:T(128)S(1)} %broadcast_clamp_fusion.1.block_ref, s32[2]{0:T(128)S(1)} %and_convert_fusion.1.valid_ref, s32[10]{0:T(128)S(1)} %slice.40.label_ref, bf16[4,25,128,512]{3,2,1,0:T(8,128)(2,1)S(1)} %copy-done.4, ...), custom_call_target="tpu_custom_call", output_to_operand_aliasing={{}: (8, {})} | custom-call | tf_op jit(solution)/shard_map/pallas_call | solution.py:79
  85.8 1.0 collective-permute-done.3.refs_1_
  86.8 5.3 %collective-permute-start.6 = (bf16[10,128,256]{2,1,0:T(8,128)(2,1)S(1)}, bf16[10,128,256]{2,1,0:T(8,128)(2,1)}, u32[]{:S(2)}, u32[]{:S(2)}) collective-permute-start(bf16[10,128,256]{2,1,0:T(8,128)(2,1)S(1)} %collective-permute-done.2.refs_0_), channel_id=1, source_target_pairs={{0,4},{4,8},{8,12},{1,5},{5,9},{9,13},{2,6},{6,10},{10,14},{3,7},{... | collective-permute-start | bytes 1966088 | tf_op jit(solution)/shard_map/ppermute | solution.py:143
  92.1 1.3 collective-permute-start.7
  93.7 4.7 %copy-done.5 = bf16[4,25,128,512]{3,2,1,0:T(8,128)(2,1)S(1)} copy-done((bf16[4,25,128,512]{3,2,1,0:T(8,128)(2,1)S(1)}, bf16[4,25,128,512]{3,2,1,0:T(8,128)(2,1)}, u32[]{:S(2)}) %copy-start.5) | copy-done | bytes 13107224
  98.4 3.1 %shard_map.77.refs_4_ = f32[512,256]{1,0:T(8,128)S(1)} custom-call(s32[2]{0:T(128)S(1)} %broadcast_clamp_fusion.block_ref, s32[2]{0:T(128)S(1)} %and_convert_fusion.valid_ref, s32[15]{0:T(128)S(1)} %bitcast.35, bf16[4,25,128,512]{3,2,1,0:T(8,128)(2,1)S(1)} %copy-done.5, ...), custom_call_target="tpu_custom_call", output_to_operand_aliasing={{}: (8, {})} | custom-call | tf_op jit(solution)/shard_map/pallas_call | solution.py:79
  101.5 0.8 collective-permute-done.10.refs_0_
  102.3 5.5 %collective-permute-done.11.refs_1_ = bf16[15,128,256]{2,1,0:T(8,128)(2,1)} collective-permute-done((bf16[15,128,256]{2,1,0:T(8,128)(2,1)S(1)}, bf16[15,128,256]{2,1,0:T(8,128)(2,1)}, u32[]{:S(2)}, u32[]{:S(2)}) %collective-permute-start.11) | collective-permute-done | bytes 983072 | tf_op jit(solution)/shard_map/ppermute | solution.py:144
  107.8 4.7 %copy-done.6 = bf16[4,25,128,512]{3,2,1,0:T(8,128)(2,1)S(1)} copy-done((bf16[4,25,128,512]{3,2,1,0:T(8,128)(2,1)S(1)}, bf16[4,25,128,512]{3,2,1,0:T(8,128)(2,1)}, u32[]{:S(2)}) %copy-start.6) | copy-done | bytes 13107224
  112.6 3.5 %shard_map.78.refs_4_ = f32[512,256]{1,0:T(8,128)S(1)} custom-call(s32[2]{0:T(128)S(1)} %broadcast_clamp_fusion.block_ref, s32[2]{0:T(128)S(1)} %and_convert_fusion.valid_ref, s32[10]{0:T(128)S(1)} %slice.40.label_ref, bf16[4,25,128,512]{3,2,1,0:T(8,128)(2,1)S(1)} %copy-done.6, ...), custom_call_target="tpu_custom_call", output_to_operand_aliasing={{}: (8, {})} | custom-call | tf_op jit(solution)/shard_map/pallas_call | solution.py:79
  116.1 4.3 %collective-permute-done.7.refs_1_ = bf16[10,128,256]{2,1,0:T(8,128)(2,1)} collective-permute-done((bf16[10,128,256]{2,1,0:T(8,128)(2,1)}, bf16[10,128,256]{2,1,0:T(8,128)(2,1)}, u32[]{:S(2)}, u32[]{:S(2)}) %collective-permute-start.7) | collective-permute-done | bytes 655392 | tf_op jit(solution)/shard_map/ppermute | solution.py:144
  120.4 4.7 %copy-done.7 = bf16[4,25,128,512]{3,2,1,0:T(8,128)(2,1)S(1)} copy-done((bf16[4,25,128,512]{3,2,1,0:T(8,128)(2,1)S(1)}, bf16[4,25,128,512]{3,2,1,0:T(8,128)(2,1)}, u32[]{:S(2)}) %copy-start.7) | copy-done | bytes 13107224
  125.2 6.0 %shard_map.79.refs_4_ = f32[512,256]{1,0:T(8,128)S(1)} custom-call(s32[2]{0:T(128)S(1)} %broadcast_clamp_fusion.2.block_ref, s32[2]{0:T(128)S(1)} %and_convert_fusion.2.valid_ref, s32[15]{0:T(128)S(1)} %bitcast.36, bf16[4,25,128,512]{3,2,1,0:T(8,128)(2,1)S(1)} %copy-done.7, ...), custom_call_target="tpu_custom_call", output_to_operand_aliasing={{}: (8, {})} | custom-call | tf_op jit(solution)/shard_map/pallas_call | solution.py:79
  131.2 3.7 %shard_map.80 = f32[512,256]{1,0:T(8,128)S(1)} custom-call(s32[2]{0:T(128)S(1)} %broadcast_clamp_fusion.2.block_ref, s32[2]{0:T(128)S(1)} %and_convert_fusion.2.valid_ref, s32[10]{0:T(128)S(1)} %slice.40.label_ref, bf16[4,25,128,512]{3,2,1,0:T(8,128)(2,1)S(1)} %copy-done.8, ...), custom_call_target="tpu_custom_call", output_to_operand_aliasing={{}: (8, {})} | custom-call | tf_op jit(solution)/shard_map/pallas_call | solution.py:79
  136.0 0.7 collective-permute-done.12
  138.2 4.2 %collective-permute-done.13 = f32[2,128,128]{1,0,2:T(2,128)S(1)} collective-permute-done((f32[2,128,128]{1,0,2:T(2,128)S(1)}, f32[2,128,128]{1,0,2:T(2,128)S(1)}, u32[]{:S(2)}, u32[]{:S(2)}) %collective-permute-start.13) | collective-permute-done | bytes 131104 | tf_op jit(solution)/shard_map/ppermute | solution.py:159
  143.1 3.2 %collective-permute-start.15 = (f32[2,128,128]{1,0,2:T(2,128)S(1)}, f32[2,128,128]{1,0,2:T(2,128)S(1)}, u32[]{:S(2)}, u32[]{:S(2)}) collective-permute-start(f32[2,128,128]{1,0,2:T(2,128)S(1)} %dynamic-slice_add_fusion), channel_id=1, source_target_pairs={{0,0},{1,4},{2,8},{3,12},{4,1},{5,5},{6,9},{7,13},{8,2},{9,6},{10,... | collective-permute-start | bytes 393224 | tf_op jit(solution)/shard_map/ppermute | solution.py:161
  146.3 3.4 %collective-permute-done.14 = f32[2,128,128]{1,0,2:T(2,128)S(1)} collective-permute-done((f32[2,128,128]{1,0,2:T(2,128)S(1)}, f32[2,128,128]{1,0,2:T(2,128)S(1)}, u32[]{:S(2)}, u32[]{:S(2)}) %collective-permute-start.14) | collective-permute-done | bytes 131104 | tf_op jit(solution)/shard_map/ppermute | solution.py:162
  149.7 3.2 %collective-permute-done.15 = f32[2,128,128]{1,0,2:T(2,128)S(1)} collective-permute-done((f32[2,128,128]{1,0,2:T(2,128)S(1)}, f32[2,128,128]{1,0,2:T(2,128)S(1)}, u32[]{:S(2)}, u32[]{:S(2)}) %collective-permute-start.15) | collective-permute-done | bytes 131104 | tf_op jit(solution)/shard_map/ppermute | solution.py:161
  153.0 1.0 fusion.1
  (54 shorter events, 4.7 us)
Async XLA Ops:
  0.0 2.8 %copy-start = (s32[100,8]{0,1:T(8,128)S(1)}, s32[100,8]{0,1:T(8,128)}, u32[]{:S(2)}) copy-start(s32[100,8]{0,1:T(8,128)} %param.11) | copy-start | bytes 9604
  6.2 12.8 %copy-start.11 = (s32[100]{0:T(128)S(1)}, s32[100]{0:T(128)}, u32[]{:S(2)}) copy-start(s32[100]{0:T(128)} %param.9) | copy-start | bytes 1204
  6.2 13.7 %copy-start.9 = (s32[512]{0:T(512)S(1)}, s32[512]{0:T(512)}, u32[]{:S(2)}) copy-start(s32[512]{0:T(512)} %param.10) | copy-start | bytes 6148
  6.5 25.6 %collective-permute-start.4 = (bf16[15,128,256]{2,1,0:T(8,128)(2,1)S(1)}, bf16[15,128,256]{2,1,0:T(8,128)(2,1)}, u32[]{:S(2)}, u32[]{:S(2)}) collective-permute-start(bf16[15,128,256]{2,1,0:T(8,128)(2,1)S(1)} %slice.51.refs_0_), channel_id=1, source_target_pairs={{0,4},{4,8},{8,12},{1,5},{5,9},{9,13},{2,6},{6,10},{10,14},{3,7},{... | collective-permute-start | bytes 2949128 | tf_op jit(solution)/shard_map/ppermute | solution.py:143
  11.0 26.7 %collective-permute-start.5 = (bf16[15,128,256]{2,1,0:T(8,128)(2,1)S(1)}, bf16[15,128,256]{2,1,0:T(8,128)(2,1)}, u32[]{:S(2)}, u32[]{:S(2)}) collective-permute-start(bf16[15,128,256]{2,1,0:T(8,128)(2,1)S(1)} %slice.51.refs_0_), channel_id=1, source_target_pairs={{4,0},{8,4},{12,8},{5,1},{9,5},{13,9},{6,2},{10,6},{14,10},{7,3},{... | collective-permute-start | bytes 2949128 | tf_op jit(solution)/shard_map/ppermute | solution.py:144
  12.3 33.9 %collective-permute-start = (bf16[10,128,256]{2,1,0:T(8,128)(2,1)S(1)}, bf16[10,128,256]{2,1,0:T(8,128)(2,1)}, u32[]{:S(2)}, u32[]{:S(2)}) collective-permute-start(bf16[10,128,256]{2,1,0:T(8,128)(2,1)S(1)} %slice.50.refs_0_), channel_id=1, source_target_pairs={{0,4},{4,8},{8,12},{1,5},{5,9},{9,13},{2,6},{6,10},{10,14},{3,7},{... | collective-permute-start | bytes 1966088 | tf_op jit(solution)/shard_map/ppermute | solution.py:143
  17.7 34.0 %collective-permute-start.1 = (bf16[10,128,256]{2,1,0:T(8,128)(2,1)S(1)}, bf16[10,128,256]{2,1,0:T(8,128)(2,1)}, u32[]{:S(2)}, u32[]{:S(2)}) collective-permute-start(bf16[10,128,256]{2,1,0:T(8,128)(2,1)S(1)} %slice.50.refs_0_), channel_id=1, source_target_pairs={{4,0},{8,4},{12,8},{5,1},{9,5},{13,9},{6,2},{10,6},{14,10},{7,3},{... | collective-permute-start | bytes 1966088 | tf_op jit(solution)/shard_map/ppermute | solution.py:144
  19.9 4.7 %copy-start.1 = (bf16[4,25,128,512]{3,2,1,0:T(8,128)(2,1)S(1)}, bf16[4,25,128,512]{3,2,1,0:T(8,128)(2,1)}, u32[]{:S(2)}) copy-start(bf16[4,25,128,512]{3,2,1,0:T(8,128)(2,1)} %amp_ref.15) | copy-start | bytes 39321604
  24.6 16.9 %copy-start.2 = (bf16[4,25,128,512]{3,2,1,0:T(8,128)(2,1)S(1)}, bf16[4,25,128,512]{3,2,1,0:T(8,128)(2,1)}, u32[]{:S(2)}) copy-start(bf16[4,25,128,512]{3,2,1,0:T(8,128)(2,1)} %amp_ref.15) | copy-start | bytes 39321604
  37.6 29.7 %collective-permute-start.8 = (bf16[15,128,256]{2,1,0:T(8,128)(2,1)}, bf16[15,128,256]{2,1,0:T(8,128)(2,1)S(1)}, u32[]{:S(2)}, u32[]{:S(2)}) collective-permute-start(bf16[15,128,256]{2,1,0:T(8,128)(2,1)} %collective-permute-done.4.refs_0_), channel_id=1, source_target_pairs={{0,4},{4,8},{8,12},{1,5},{5,9},{9,13},{2,6},{6,10},{10,14},{3,7},{... | collective-permute-start | bytes 2949128 | tf_op jit(solution)/shard_map/ppermute | solution.py:143
  40.2 32.4 %collective-permute-start.9 = (bf16[15,128,256]{2,1,0:T(8,128)(2,1)}, bf16[15,128,256]{2,1,0:T(8,128)(2,1)S(1)}, u32[]{:S(2)}, u32[]{:S(2)}) collective-permute-start(bf16[15,128,256]{2,1,0:T(8,128)(2,1)} %collective-permute-done.5.refs_1_), channel_id=1, source_target_pairs={{4,0},{8,4},{12,8},{5,1},{9,5},{13,9},{6,2},{10,6},{14,10},{7,3},{... | collective-permute-start | bytes 2949128 | tf_op jit(solution)/shard_map/ppermute | solution.py:144
  51.7 34.1 %collective-permute-start.2 = (bf16[10,128,256]{2,1,0:T(8,128)(2,1)}, bf16[10,128,256]{2,1,0:T(8,128)(2,1)S(1)}, u32[]{:S(2)}, u32[]{:S(2)}) collective-permute-start(bf16[10,128,256]{2,1,0:T(8,128)(2,1)} %collective-permute-done.refs_0_), channel_id=1, source_target_pairs={{0,4},{4,8},{8,12},{1,5},{5,9},{9,13},{2,6},{6,10},{10,14},{3,7},{... | collective-permute-start | bytes 1966088 | tf_op jit(solution)/shard_map/ppermute | solution.py:143
  54.2 32.6 %collective-permute-start.3 = (bf16[10,128,256]{2,1,0:T(8,128)(2,1)}, bf16[10,128,256]{2,1,0:T(8,128)(2,1)}, u32[]{:S(2)}, u32[]{:S(2)}) collective-permute-start(bf16[10,128,256]{2,1,0:T(8,128)(2,1)} %collective-permute-done.1.refs_1_), channel_id=1, source_target_pairs={{4,0},{8,4},{12,8},{5,1},{9,5},{13,9},{6,2},{10,6},{14,10},{7,3},{... | collective-permute-start | bytes 1966088 | tf_op jit(solution)/shard_map/ppermute | solution.py:144
  55.7 4.7 %copy-start.3 = (bf16[4,25,128,512]{3,2,1,0:T(8,128)(2,1)S(1)}, bf16[4,25,128,512]{3,2,1,0:T(8,128)(2,1)}, u32[]{:S(2)}) copy-start(bf16[4,25,128,512]{3,2,1,0:T(8,128)(2,1)} %amp_ref.15) | copy-start | bytes 39321604
  72.6 29.7 %collective-permute-start.10 = (bf16[15,128,256]{2,1,0:T(8,128)(2,1)S(1)}, bf16[15,128,256]{2,1,0:T(8,128)(2,1)}, u32[]{:S(2)}, u32[]{:S(2)}) collective-permute-start(bf16[15,128,256]{2,1,0:T(8,128)(2,1)S(1)} %collective-permute-done.8.refs_0_), channel_id=1, source_target_pairs={{0,4},{4,8},{8,12},{1,5},{5,9},{9,13},{2,6},{6,10},{10,14},{3,7},{... | collective-permute-start | bytes 2949128 | tf_op jit(solution)/shard_map/ppermute | solution.py:143
  76.1 31.7 %collective-permute-start.11 = (bf16[15,128,256]{2,1,0:T(8,128)(2,1)S(1)}, bf16[15,128,256]{2,1,0:T(8,128)(2,1)}, u32[]{:S(2)}, u32[]{:S(2)}) collective-permute-start(bf16[15,128,256]{2,1,0:T(8,128)(2,1)S(1)} %collective-permute-done.9.refs_1_), channel_id=1, source_target_pairs={{4,0},{8,4},{12,8},{5,1},{9,5},{13,9},{6,2},{10,6},{14,10},{7,3},{... | collective-permute-start | bytes 2949128 | tf_op jit(solution)/shard_map/ppermute | solution.py:144
  77.4 4.7 %copy-start.4 = (bf16[4,25,128,512]{3,2,1,0:T(8,128)(2,1)S(1)}, bf16[4,25,128,512]{3,2,1,0:T(8,128)(2,1)}, u32[]{:S(2)}) copy-start(bf16[4,25,128,512]{3,2,1,0:T(8,128)(2,1)} %amp_ref.15) | copy-start | bytes 39321604
  86.8 29.3 %collective-permute-start.6 = (bf16[10,128,256]{2,1,0:T(8,128)(2,1)S(1)}, bf16[10,128,256]{2,1,0:T(8,128)(2,1)}, u32[]{:S(2)}, u32[]{:S(2)}) collective-permute-start(bf16[10,128,256]{2,1,0:T(8,128)(2,1)S(1)} %collective-permute-done.2.refs_0_), channel_id=1, source_target_pairs={{0,4},{4,8},{8,12},{1,5},{5,9},{9,13},{2,6},{6,10},{10,14},{3,7},{... | collective-permute-start | bytes 1966088 | tf_op jit(solution)/shard_map/ppermute | solution.py:143
  92.1 28.3 %collective-permute-start.7 = (bf16[10,128,256]{2,1,0:T(8,128)(2,1)}, bf16[10,128,256]{2,1,0:T(8,128)(2,1)}, u32[]{:S(2)}, u32[]{:S(2)}) collective-permute-start(bf16[10,128,256]{2,1,0:T(8,128)(2,1)} %collective-permute-done.3.refs_1_), channel_id=1, source_target_pairs={{4,0},{8,4},{12,8},{5,1},{9,5},{13,9},{6,2},{10,6},{14,10},{7,3},{... | collective-permute-start | bytes 1966088 | tf_op jit(solution)/shard_map/ppermute | solution.py:144
  93.7 4.7 %copy-start.5 = (bf16[4,25,128,512]{3,2,1,0:T(8,128)(2,1)S(1)}, bf16[4,25,128,512]{3,2,1,0:T(8,128)(2,1)}, u32[]{:S(2)}) copy-start(bf16[4,25,128,512]{3,2,1,0:T(8,128)(2,1)} %amp_ref.15) | copy-start | bytes 39321604
  107.8 4.7 %copy-start.6 = (bf16[4,25,128,512]{3,2,1,0:T(8,128)(2,1)S(1)}, bf16[4,25,128,512]{3,2,1,0:T(8,128)(2,1)}, u32[]{:S(2)}) copy-start(bf16[4,25,128,512]{3,2,1,0:T(8,128)(2,1)} %amp_ref.15) | copy-start | bytes 39321604
  120.4 4.7 %copy-start.7 = (bf16[4,25,128,512]{3,2,1,0:T(8,128)(2,1)S(1)}, bf16[4,25,128,512]{3,2,1,0:T(8,128)(2,1)}, u32[]{:S(2)}) copy-start(bf16[4,25,128,512]{3,2,1,0:T(8,128)(2,1)} %amp_ref.15) | copy-start | bytes 39321604
  125.2 6.0 %copy-start.8 = (bf16[4,25,128,512]{3,2,1,0:T(8,128)(2,1)S(1)}, bf16[4,25,128,512]{3,2,1,0:T(8,128)(2,1)}, u32[]{:S(2)}) copy-start(bf16[4,25,128,512]{3,2,1,0:T(8,128)(2,1)} %amp_ref.15) | copy-start | bytes 39321604
  131.2 4.0 %copy-start.12 = (f32[100]{0:T(128)S(1)}, f32[100]{0:T(128)}, u32[]{:S(2)}) copy-start(f32[100]{0:T(128)} %param.12) | copy-start | bytes 1204
  131.2 6.9 %copy-start.10 = (f32[512]{0:T(512)S(1)}, f32[512]{0:T(512)}, u32[]{:S(2)}) copy-start(f32[512]{0:T(512)} %param.13) | copy-start | bytes 6148
  135.1 1.6 %collective-permute-start.12 = (f32[4,128,128]{1,0,2:T(4,128)S(1)}, f32[4,128,128]{1,0,2:T(4,128)S(1)}, u32[]{:S(2)}, u32[]{:S(2)}) collective-permute-start(f32[4,128,128]{1,0,2:T(4,128)S(1)} %copy.42), channel_id=1, source_target_pairs={{0,1},{1,0},{2,3},{3,2},{4,5},{5,4},{6,7},{7,6},{8,9},{9,8},{10,11... | collective-permute-start | bytes 786440 | tf_op jit(solution)/shard_map/ppermute | solution.py:155
  136.8 5.6 %collective-permute-start.13 = (f32[2,128,128]{1,0,2:T(2,128)S(1)}, f32[2,128,128]{1,0,2:T(2,128)S(1)}, u32[]{:S(2)}, u32[]{:S(2)}) collective-permute-start(f32[2,128,128]{1,0,2:T(2,128)S(1)} %constant_dynamic-slice_fusion), channel_id=1, source_target_pairs={{0,2},{1,3},{2,0},{3,1},{4,6},{5,7},{6,4},{7,5},{8,10},{9,11},{10,... | collective-permute-start | bytes 393224 | tf_op jit(solution)/shard_map/ppermute | solution.py:159
  142.5 7.2 %collective-permute-start.14 = (f32[2,128,128]{1,0,2:T(2,128)S(1)}, f32[2,128,128]{1,0,2:T(2,128)S(1)}, u32[]{:S(2)}, u32[]{:S(2)}) collective-permute-start(f32[2,128,128]{1,0,2:T(2,128)S(1)} %dynamic-slice_add_fusion), channel_id=1, source_target_pairs={{0,8},{1,12},{2,0},{3,4},{4,9},{5,13},{6,1},{7,5},{8,10},{9,14},{1... | collective-permute-start | bytes 393224 | tf_op jit(solution)/shard_map/ppermute | solution.py:162
  143.1 9.9 %collective-permute-start.15 = (f32[2,128,128]{1,0,2:T(2,128)S(1)}, f32[2,128,128]{1,0,2:T(2,128)S(1)}, u32[]{:S(2)}, u32[]{:S(2)}) collective-permute-start(f32[2,128,128]{1,0,2:T(2,128)S(1)} %dynamic-slice_add_fusion), channel_id=1, source_target_pairs={{0,0},{1,4},{2,8},{3,12},{4,1},{5,5},{6,9},{7,13},{8,2},{9,6},{10,... | collective-permute-start | bytes 393224 | tf_op jit(solution)/shard_map/ppermute | solution.py:161
